TPU v7x, 128 devices: a whole 4x4x4 slice. The times are simulated.
128 devices in a mesh: dp: 16 (over y_lo, x, core), ctx: 8 (over y_hi, z).
Axes of the slice: x: 4, y: 4 (y_hi: 2, y_lo: 2; y = y_hi * 2 + y_lo), z: 4, core: 2. Of those that a mesh axis runs over, the one named last changes fastest.
Arguments:
- tokens: bfloat16 [16, 3072, 4096], P('dp', 'ctx'), may hold values from -64 to 64
- positions: int32 [16, 3072], P('dp', 'ctx'), may hold values from 0 to 3071, each once within a row
- segment_ids: int32 [16, 3072], P('dp'), may hold values from 0 to 7, never falling along the last dimension, each value on 1 to 1536 neighbouring positions
- w_query: bfloat16 [4096, 2048], P('dp'), may hold values from -0.09375 to 0.09375
- key_weight: bfloat16 [4096, 512], P('dp'), may hold values from -0.09375 to 0.09375
- value_weight: bfloat16 [4096, 512], P('dp'), may hold values from -0.09375 to 0.09375
Outputs:
- attended: bfloat16 [16, 3072, 2048], P('dp', 'ctx')
Inputs may be any that keep to these rules, and one draw needn't show every extreme that they name: Each row is a permutation of the positions of its sequence. `segment_ids`: never falling along positions; each document 1 to 1536 positions.
All inputs are finite; a program needn't handle non-finite values.
Results may differ from a plain program's by a relative error of at most 0.017.
The roundings to bfloat16 on the way count: a program that leaves them out, or rounds other values in their place, can miss the bound.
Values may be sent and summed in bfloat16 or wider, within the bound.
A program may use at most 128 MiB of HBM per device.

v0:
```python
import math

import jax
import jax.numpy as jnp
from jax import lax
from jax.sharding import PartitionSpec as P

QUERY_HEADS = 16
KEY_VALUE_HEADS = 4
HEAD_SIZE = 128


def apply_rotary(mat, token_position, heads):
    half = HEAD_SIZE // 2
    freq = 500000.0 ** (-jnp.arange(half, dtype=jnp.float32) / half)
    angle = token_position.astype(jnp.float32)[:, None] * freq[None, :]
    cosine = jnp.cos(angle)[:, None, :]
    sine = jnp.sin(angle)[:, None, :]
    split = mat.reshape(mat.shape[0], heads, HEAD_SIZE)
    first = split[..., :half]
    second = split[..., half:]
    turned = jnp.concatenate(
        [first * cosine - second * sine, second * cosine + first * sine], axis=-1
    )
    return turned.reshape(mat.shape[0], heads * HEAD_SIZE)


def shards(tokens, positions, segment_ids, w_query, key_weight, value_weight):
    sequence_list, token_rows, width = tokens.shape
    flat = tokens.reshape(sequence_list * token_rows, width)
    query_group = QUERY_HEADS // KEY_VALUE_HEADS
    part = flat
    query_projected = jnp.dot(
        part, lax.all_gather(w_query, "dp", axis=0, tiled=True), preferred_element_type=jnp.float32
    )
    pieces = (
        lax.all_gather(key_weight, "dp", axis=0, tiled=True),
        lax.all_gather(value_weight, "dp", axis=0, tiled=True),
    )
    part = flat
    key_projected, value_projected = tuple(
        (jnp.dot(part, p, preferred_element_type=jnp.float32) for p in pieces)
    )
    flat_positions = positions.reshape(-1)
    query_matrix = (
        apply_rotary(query_projected, flat_positions, QUERY_HEADS)
        .astype(jnp.bfloat16)
        .reshape(sequence_list, token_rows, KEY_VALUE_HEADS, query_group, HEAD_SIZE)
    )
    key = (
        apply_rotary(key_projected, flat_positions, KEY_VALUE_HEADS)
        .astype(jnp.bfloat16)
        .reshape(sequence_list, token_rows, KEY_VALUE_HEADS * HEAD_SIZE)
    )
    value_matrix = value_projected.astype(jnp.bfloat16).reshape(
        sequence_list, token_rows, KEY_VALUE_HEADS * HEAD_SIZE
    )
    seg = jnp.take_along_axis(segment_ids, positions, axis=1)
    factor = HEAD_SIZE ** (-0.5)
    start_state = (
        jnp.full((sequence_list, KEY_VALUE_HEADS, query_group, token_rows), -1e30, jnp.float32),
        jnp.zeros((sequence_list, KEY_VALUE_HEADS, query_group, token_rows), jnp.float32),
        jnp.zeros(
            (sequence_list, token_rows, KEY_VALUE_HEADS, query_group, HEAD_SIZE), jnp.float32
        ),
    )
    key_rows = lax.all_gather(key, "ctx", axis=1, tiled=True)
    values = lax.all_gather(value_matrix, "ctx", axis=1, tiled=True)
    key_pos = lax.all_gather(positions, "ctx", axis=1, tiled=True)
    key_seg = lax.all_gather(seg, "ctx", axis=1, tiled=True)
    count = key_rows.shape[1]
    attention_block = math.gcd(count, 256)
    steps = count // attention_block

    def one_block(index, state):
        top, total, summed = state
        k_block = lax.dynamic_slice_in_dim(
            key_rows, index * attention_block, attention_block, 1
        ).reshape(sequence_list, attention_block, KEY_VALUE_HEADS, HEAD_SIZE)
        v_block = lax.dynamic_slice_in_dim(
            values, index * attention_block, attention_block, 1
        ).reshape(sequence_list, attention_block, KEY_VALUE_HEADS, HEAD_SIZE)
        p_block = lax.dynamic_slice_in_dim(key_pos, index * attention_block, attention_block, 1)
        s_block = lax.dynamic_slice_in_dim(key_seg, index * attention_block, attention_block, 1)
        score = (
            jnp.einsum(
                "sqhgd,skhd->shgqk", query_matrix, k_block, preferred_element_type=jnp.float32
            )
            * factor
        )
        visible = (p_block[:, None, :] <= positions[:, :, None]) & (
            s_block[:, None, :] == seg[:, :, None]
        )
        visible = visible[:, None, None]
        score = jnp.where(visible, score, -1e30)
        new_top = jnp.maximum(top, jnp.max(score, axis=-1))
        expo = jnp.where(visible, jnp.exp(score - new_top[..., None]), 0.0)
        fade = jnp.exp(top - new_top)
        total = total * fade + jnp.sum(expo, axis=-1)
        added = jnp.einsum(
            "shgqk,skhd->sqhgd",
            expo.astype(jnp.bfloat16),
            v_block,
            preferred_element_type=jnp.float32,
        )
        summed = summed * fade.transpose(0, 3, 1, 2)[..., None] + added
        return (new_top, total, summed)

    top, total, summed = lax.fori_loop(0, steps, one_block, start_state)
    result = summed / total.transpose(0, 3, 1, 2)[..., None]
    return result.reshape(sequence_list, token_rows, QUERY_HEADS * HEAD_SIZE).astype(jnp.bfloat16)


def solution(mesh):
    placed = (
        P("dp", "ctx", None),
        P("dp", "ctx"),
        P("dp", None),
        P("dp", None),
        P("dp", None),
        P("dp", None),
    )
    return jax.shard_map(
        shards, mesh=mesh, in_specs=placed, out_specs=P("dp", "ctx", None), check_vma=False
    )
```

profile of v0, /device:TPU:1, one launch (start us, length us, event | category | flops | bytes accessed | tf_op | source)
XLA Modules:
  0.0 435.5 jit_solution(16795312100841371301)
XLA Ops:
  8.8 41.2 %all-gather.13.cloned.1.call-done = bf16[4096,512]{1,0:T(8,128)(2,1)} async-done(((bf16[256,512]{1,0:T(8,128)(2,1)}), bf16[4096,512]{1,0:T(8,128)(2,1)}) %all-gather.13.cloned.1.call-update) | async-done | bytes 4194320 | tf_op jit(solution)/shard_map/all_gather | solution.py:38
  50.0 4.7 %fusion.25 = bf16[384,512]{1,0:T(8,128)(2,1)} fusion(bf16[4096,512]{1,0:T(8,128)(2,1)} %all-gather.13.cloned.1.call-done, bf16[1,384,4096]{2,1,0:T(8,128)(2,1)S(1)} %copy-done), kind=kOutput, calls=%fused_computation.40 | convolution fusion | flops 1610809344 | bytes 7733248 | tf_op jit(solution)/shard_map/dot_general | solution.py:42
  55.3 33.9 %all-gather.7.cloned.1.call-done = bf16[4096,512]{1,0:T(8,128)(2,1)} async-done(((bf16[256,512]{1,0:T(8,128)(2,1)}), bf16[4096,512]{1,0:T(8,128)(2,1)}) %all-gather.7.cloned.1.call-update) | async-done | bytes 4194320 | tf_op jit(solution)/shard_map/all_gather | solution.py:37
  89.2 6.5 %copy.16 = bf16[512,4096]{1,0:T(8,128)(2,1)} copy(bf16[512,4096]{0,1:T(8,128)(2,1)} %bitcast.119) | data formatting | bytes 8388608 | tf_op jit(solution)/shard_map/dot_general | solution.py:42
  95.6 4.5 %fusion.21 = f32[384,4,128]{0,2,1:T(8,128)S(1)} fusion(bf16[4,128,4096]{2,1,0:T(8,128)(2,1)} %bitcast.120, bf16[1,384,4096]{2,1,0:T(8,128)(2,1)S(1)} %copy-done), kind=kOutput, calls=%fused_computation.32 | convolution fusion | flops 1610612736 | bytes 8126464 | tf_op jit(solution)/shard_map/dot_general | solution.py:42
  101.2 2.5 gather_fusion
  103.7 25.2 %all_gather.21 = s32[1,3072]{1,0:T(1,128)S(1)} all-gather(s32[1,384]{1,0:T(1,128)S(1)} %copy-done.5), channel_id=1, replica_groups=mesh['dp'=16,'ctx'=8] {'ctx'}, dimensions={1}, use_global_device_ids=true | all-gather | bytes 13824 | tf_op jit(solution)/shard_map/all_gather | solution.py:69
  129.0 25.2 %all_gather.22 = s32[1,3072]{1,0:T(1,128)S(1)} all-gather(s32[1,384]{1,0:T(1,128)S(1)} %and_select_fusion), channel_id=1, replica_groups=mesh['dp'=16,'ctx'=8] {'ctx'}, dimensions={1}, use_global_device_ids=true | all-gather | bytes 13824 | tf_op jit(solution)/shard_map/all_gather | solution.py:70
  154.2 28.4 %all-gather.11.cloned.1.call-done = bf16[4096,2048]{1,0:T(8,128)(2,1)} async-done(((bf16[256,2048]{1,0:T(8,128)(2,1)}), bf16[4096,2048]{1,0:T(8,128)(2,1)}) %all-gather.11.cloned.1.call-update) | async-done | bytes 16777232 | tf_op jit(solution)/shard_map/all_gather | solution.py:34
  182.6 20.8 %copy.17 = bf16[2048,4096]{1,0:T(8,128)(2,1)} copy(bf16[2048,4096]{0,1:T(8,128)(2,1)} %bitcast.112) | data formatting | bytes 33554432 | tf_op jit(solution)/shard_map/dot_general | solution.py:33
  203.4 11.6 %fusion.19 = f32[384,16,128]{0,2,1:T(8,128)S(1)} fusion(bf16[16,128,4096]{2,1,0:T(8,128)(2,1)} %bitcast.113, bf16[1,384,4096]{2,1,0:T(8,128)(2,1)S(1)} %copy-done), kind=kOutput, calls=%fused_computation.30 | convolution fusion | flops 6442450944 | bytes 23068672 | tf_op jit(solution)/shard_map/dot_general | solution.py:33
  216.7 30.9 %all-gather.15.cloned.1.call-done = bf16[3072,512]{1,0:T(8,128)(2,1)} async-done(((bf16[384,512]{1,0:T(8,128)(2,1)}), bf16[3072,512]{1,0:T(8,128)(2,1)}) %all-gather.15.cloned.1.call-update) | async-done | bytes 3145744 | tf_op jit(solution)/shard_map/all_gather | solution.py:68
  247.6 63.9 %all-gather.9.cloned.1.call-done = bf16[1,3072,512]{1,2,0:T(8,128)(2,1)} async-done(((bf16[1,384,512]{1,2,0:T(8,128)(2,1)}), bf16[1,3072,512]{1,2,0:T(8,128)(2,1)}) %all-gather.9.cloned.1.call-update) | async-done | bytes 3145744 | tf_op jit(solution)/shard_map/all_gather | solution.py:67
  311.5 111.4 %while.18 = (s32[]{:T(128)}, f32[1,4,4,384]{3,2,1,0:T(4,128)S(1)}, f32[1,4,4,384]{3,2,1,0:T(4,128)S(1)}, f32[1,384,4,4,128]{1,4,3,2,0:T(8,128)}, s32[1,3072]{1,0...) while((s32[]{:T(128)}, f32[1,4,4,384]{3,2,1,0:T(4,128)S(1)}, ...), condition=%wide.region_3.4_spmd.clone, body=%wide.region_0.3_spmd.clone.sunk | while | flops 828444672 | bytes 54803736 | solution.py:109
  316.9 2.1 bitcast_add_fusion.5
  319.1 1.6 copy-done.4
  326.2 2.1 bitcast_add_fusion.5
  328.4 1.6 copy-done.4
  335.5 2.1 bitcast_add_fusion.5
  337.7 1.6 copy-done.4
  344.8 2.1 bitcast_add_fusion.5
  347.0 1.6 copy-done.4
  354.0 2.1 bitcast_add_fusion.5
  363.3 2.1 bitcast_add_fusion.5
  372.6 2.1 bitcast_add_fusion.5
  381.9 2.1 bitcast_add_fusion.5
  391.2 2.1 bitcast_add_fusion.5
  400.4 2.1 bitcast_add_fusion.5
  409.7 2.1 bitcast_add_fusion.5
  419.0 2.1 bitcast_add_fusion.5
  422.8 3.5 divide_convert_fusion
  426.4 2.6 copy.24
  (220 shorter events, 83.7 us)
Async XLA Ops:
  6.5 43.5 %copy-start = (bf16[1,384,4096]{2,1,0:T(8,128)(2,1)S(1)}, bf16[1,384,4096]{2,1,0:T(8,128)(2,1)}, u32[]{:S(2)}) copy-start(bf16[1,384,4096]{2,1,0:T(8,128)(2,1)} %param.8) | copy-start | bytes 9437188
  6.5 43.5 %all-gather.13.cloned.1.call-start = ((), (), s32[]{:S(2)}) async-start(), calls=%async_computation.3 | async-start | bytes 4456448 | tf_op jit(solution)/shard_map/all_gather | solution.py:38
  7.3 81.9 %all-gather.7.cloned.1.call-start = ((), (), s32[]{:S(2)}) async-start(), calls=%async_computation | async-start | bytes 4456448 | tf_op jit(solution)/shard_map/all_gather | solution.py:37
  8.0 174.6 %all-gather.11.cloned.1.call-start = ((), (), s32[]{:S(2)}) async-start(), calls=%async_computation.2 | async-start | bytes 17825792 | tf_op jit(solution)/shard_map/all_gather | solution.py:34
  8.7 46.1 %copy-start.5 = (s32[1,384]{1,0:T(1,128)S(1)}, s32[1,384]{1,0:T(1,128)}, u32[]{:S(2)}) copy-start(s32[1,384]{1,0:T(1,128)} %param.9) | copy-start | bytes 4612
  8.8 238.8 %all-gather.15.cloned.1.call-start = ((), (), s32[]{:S(2)}) async-start(), calls=%async_computation.4 | async-start | bytes 3538944 | tf_op jit(solution)/shard_map/all_gather | solution.py:68
  54.8 256.7 %all-gather.9.cloned.1.call-start = ((), (), s32[]{:S(2)}) async-start(), calls=%async_computation.1 | async-start | bytes 3538944 | tf_op jit(solution)/shard_map/all_gather | solution.py:67
  315.0 1.9 copy-start.3
  319.1 1.7 copy-start.4
  324.3 1.9 copy-start.3
  328.4 1.7 copy-start.4
  333.6 1.9 copy-start.3
  337.6 1.7 copy-start.4
  342.9 1.9 copy-start.3
  346.9 1.7 copy-start.4
  352.2 1.9 copy-start.3
  356.2 1.7 copy-start.4
  361.4 1.9 copy-start.3
  365.5 1.7 copy-start.4
  370.7 1.9 copy-start.3
  374.8 1.7 copy-start.4
  380.0 1.9 copy-start.3
  384.0 1.7 copy-start.4
  389.3 1.9 copy-start.3
  393.3 1.7 copy-start.4
  398.6 1.9 copy-start.3
  402.6 1.7 copy-start.4
  407.8 1.9 copy-start.3
  411.9 1.7 copy-start.4
  417.1 1.9 copy-start.3
  421.2 1.7 copy-start.4
  422.8 6.1 %copy-start.1 = (bf16[1,384,4096]{2,1,0:T(8,128)(2,1)S(1)}, bf16[1,384,4096]{2,1,0:T(8,128)(2,1)}, u32[]{:S(2)}) copy-start(bf16[1,384,4096]{2,1,0:T(8,128)(2,1)} %param.8) | copy-start | bytes 9437188
  (1 other events, 1.0 us)
Sparse Core Ops, SparseCore 0:
  9.1 40.9 all-gather.12
  51.7 37.3 all-gather.6
  90.9 91.6 all-gather.10
  184.7 62.7 all-gather.14
  249.6 61.7 all-gather.8
where the time goes:
time: 437 us; the launch traced here: 435 us
  waiting for transfers between devices  200 us (46%)
  local copies, waits for them, and re-layouts  81.5 us (19%)
  matrix products  61.6 us (14%)
  blocking collectives  50.4 us (12%)
  other arithmetic  27.4 us (6%)
  between operations  13.3 us (3%)
    all_gather x1, waiting for transfers between devices, shards(): key_rows = lax.all_gather(key, 'ctx', axis=1, tiled=True)  63.9 us
    all_gather x1, waiting for transfers between devices, shards(): lax.all_gather(value_weight, 'dp', axis=0, tiled=True)  41.2 us
    all_gather x1, waiting for transfers between devices, shards(): lax.all_gather(key_weight, 'dp', axis=0, tiled=True)  33.9 us
    all_gather x1, waiting for transfers between devices, shards(): values = lax.all_gather(value_matrix, 'ctx', axis=1, tiled=True)  30.9 us
    all_gather x1, waiting for transfers between devices, shards(): lax.all_gather(w_query, 'dp', axis=0, tiled=True)  28.4 us
    dot_general x12, matrix products, one_block(): jnp.einsum('shgqk,skhd->sqhgd', expo.astype(jnp.bfloat16), v_block, prefe...  25.8 us
    all_gather x1, blocking collectives, shards(): key_pos = lax.all_gather(positions, 'ctx', axis=1, tiled=True)  25.2 us
    all_gather x1, blocking collectives, shards(): key_seg = lax.all_gather(seg, 'ctx', axis=1, tiled=True)  25.2 us
  transfers between devices with their start and end apart: 5, of which 5 were waited for; matrix products, arithmetic and copies ran while one was open for 12% of the time, Pallas kernels for 0%

commit v1 on v0

v1 whole, which is shorter than its diff:
```python
import math

import jax
import jax.numpy as jnp
from jax import lax
from jax.experimental import pallas as pl
from jax.experimental.pallas import tpu as pltpu
from jax.sharding import PartitionSpec as P

QUERY_HEADS = 16
KEY_VALUE_HEADS = 4
HEAD_SIZE = 128
DOCS = 8


def apply_rotary(mat, token_position, heads):
    half = HEAD_SIZE // 2
    freq = 500000.0 ** (-jnp.arange(half, dtype=jnp.float32) / half)
    angle = token_position.astype(jnp.float32)[:, None] * freq[None, :]
    cosine = jnp.cos(angle)[:, None, :]
    sine = jnp.sin(angle)[:, None, :]
    split = mat.reshape(mat.shape[0], heads, HEAD_SIZE)
    first = split[..., :half]
    second = split[..., half:]
    turned = jnp.concatenate(
        [first * cosine - second * sine, second * cosine + first * sine], axis=-1
    )
    return turned.reshape(mat.shape[0], heads * HEAD_SIZE)


RUNS = 8
TOKENS = 384
KEY_BLOCK = 256
QUERY_TILE = 64
GROUP = 4
NEVER = -1e30


def attention_kernel(q_ref, kv_ref, runs_ref, mine_ref, stored_ref, seg_ref, out_ref, key_pos, top, total, summed, rows_done):
    part = KEY_BLOCK // RUNS
    blocks = TOKENS // part
    tiles = TOKENS // QUERY_TILE
    width = GROUP * QUERY_TILE
    factor = HEAD_SIZE ** -0.5 * math.log2(math.e)

    query_pos = mine_ref[...]
    seg = seg_ref[...]
    start = jnp.zeros_like(query_pos)
    for doc in range(1, DOCS):
        before = jnp.sum((seg < doc).astype(jnp.float32), axis=(0, 1), keepdims=True)
        start = jnp.where(before <= query_pos, jnp.maximum(start, before), start)

    runs = runs_ref[...]
    columns = runs.T
    for run in range(RUNS):
        wide = jnp.broadcast_to(columns[:, run : run + 1], (TOKENS, 128))
        key_pos[:, run] = wide.reshape(blocks, part, 128)

    lane = lax.broadcasted_iota(jnp.int32, (1, TOKENS), 1) % part
    lowest = jnp.where(lane == 0, jnp.min(runs, axis=0, keepdims=True), 1e9)
    highest = jnp.where(lane == part - 1, jnp.max(runs, axis=0, keepdims=True), 1e9)

    for tile in range(tiles):
        at = slice(tile * QUERY_TILE, (tile + 1) * QUERY_TILE)
        pos_row = jnp.concatenate([query_pos[:, at]] * GROUP, axis=1)
        start_row = jnp.concatenate([start[:, at]] * GROUP, axis=1)
        last = jnp.max(query_pos[:, at], axis=1, keepdims=True)
        first = jnp.min(start[:, at], axis=1, keepdims=True)
        begin = jnp.sum((highest < first).astype(jnp.int32))
        end = jnp.sum((lowest <= last).astype(jnp.int32))
        top[...] = jnp.full_like(top, NEVER)
        total[...] = jnp.zeros_like(total)
        summed[...] = jnp.zeros_like(summed)
        queries = [
            jnp.concatenate(
                [q_ref[at, (head * GROUP + g) * HEAD_SIZE : (head * GROUP + g + 1) * HEAD_SIZE] for g in range(GROUP)],
                axis=0,
            )
            for head in range(KEY_VALUE_HEADS)
        ]

        def one_block(block, carry):
            rows = pl.ds(pl.multiple_of(block * KEY_BLOCK, KEY_BLOCK), KEY_BLOCK)
            pos = key_pos[block].reshape(KEY_BLOCK, 128)
            pos = jnp.concatenate([pos] * (width // 128), axis=1)
            visible = (pos <= pos_row) & (pos >= start_row)
            for head in range(KEY_VALUE_HEADS):
                at_head = 2 * head * HEAD_SIZE
                keys = kv_ref[rows, at_head : at_head + HEAD_SIZE]
                values = kv_ref[rows, at_head + HEAD_SIZE : at_head + 2 * HEAD_SIZE]
                score = lax.dot_general(
                    keys, queries[head], (((1,), (1,)), ((), ())), preferred_element_type=jnp.float32
                )
                score = jnp.where(visible, score, -jnp.inf)
                old = top[head]
                new = jnp.maximum(old, jnp.max(score, axis=0, keepdims=True))
                weight = jnp.exp2((score - new) * factor)
                fade = jnp.exp2((old - new) * factor)
                top[head] = new
                total[head] = total[head] * fade + jnp.sum(weight, axis=0, keepdims=True)
                added = lax.dot_general(
                    values, weight.astype(jnp.bfloat16), (((0,), (0,)), ((), ())), preferred_element_type=jnp.float32
                )
                summed[head] = summed[head] * fade + added
            return carry

        lax.fori_loop(begin, end, one_block, 0)
        for head in range(KEY_VALUE_HEADS):
            result = (summed[head] / total[head]).astype(jnp.bfloat16)
            for g in range(GROUP):
                rows_done[head * GROUP + g, :, at] = result[:, g * QUERY_TILE : (g + 1) * QUERY_TILE]

    turn = (stored_ref[...] == query_pos).astype(jnp.bfloat16)
    for head in range(QUERY_HEADS):
        out_ref[:, head * HEAD_SIZE : (head + 1) * HEAD_SIZE] = lax.dot_general(
            turn, rows_done[head], (((1,), (1,)), ((), ())), preferred_element_type=jnp.float32
        ).astype(jnp.bfloat16)


def attention(query, kv, runs, mine, stored, seg):
    part = KEY_BLOCK // RUNS
    width = GROUP * QUERY_TILE
    return pl.pallas_call(
        attention_kernel,
        out_shape=jax.ShapeDtypeStruct((TOKENS, QUERY_HEADS * HEAD_SIZE), jnp.bfloat16),
        in_specs=[pl.BlockSpec(memory_space=pltpu.VMEM)] * 6,
        out_specs=pl.BlockSpec(memory_space=pltpu.VMEM),
        scratch_shapes=[
            pltpu.VMEM((TOKENS // part, RUNS, part, 128), jnp.float32),
            pltpu.VMEM((KEY_VALUE_HEADS, 1, width), jnp.float32),
            pltpu.VMEM((KEY_VALUE_HEADS, 1, width), jnp.float32),
            pltpu.VMEM((KEY_VALUE_HEADS, HEAD_SIZE, width), jnp.float32),
            pltpu.VMEM((QUERY_HEADS, HEAD_SIZE, TOKENS), jnp.bfloat16),
        ],
        compiler_params=pltpu.CompilerParams(vmem_limit_bytes=56 << 20),
        cost_estimate=pl.CostEstimate(flops=5 * 10**9, bytes_accessed=11 * 10**6, transcendentals=10**7),
        name="attention",
    )(query, kv, runs, mine, stored, seg)


def shards(tokens, positions, segment_ids, w_query, key_weight, value_weight):
    token_rows, width = tokens.shape[1:]
    flat = tokens.reshape(token_rows, width)
    pos = positions.reshape(-1)
    rank = jnp.sum(pos[None, :] < pos[:, None], axis=1)
    order = (rank[None, :] == jnp.arange(token_rows)[:, None])
    mine = jnp.sum(jnp.where(order, pos[None, :], 0), axis=1)
    flat = jnp.dot(order.astype(jnp.bfloat16), flat, preferred_element_type=jnp.float32).astype(jnp.bfloat16)
    query = jnp.dot(flat, lax.all_gather(w_query, "dp", axis=0, tiled=True), preferred_element_type=jnp.float32)
    both = jnp.concatenate([key_weight, value_weight], axis=1)
    both = jnp.dot(flat, lax.all_gather(both, "dp", axis=0, tiled=True), preferred_element_type=jnp.float32)
    split = KEY_VALUE_HEADS * HEAD_SIZE
    query = apply_rotary(query, mine, QUERY_HEADS).astype(jnp.bfloat16)
    key = apply_rotary(both[:, :split], mine, KEY_VALUE_HEADS).astype(jnp.bfloat16)
    value = both[:, split:].astype(jnp.bfloat16)
    kv = jnp.stack([key.reshape(-1, KEY_VALUE_HEADS, HEAD_SIZE), value.reshape(-1, KEY_VALUE_HEADS, HEAD_SIZE)], axis=2)
    kv = lax.all_gather(kv.reshape(token_rows, 2 * split), "ctx", axis=0)
    runs = lax.all_gather(mine, "ctx", axis=0).astype(jnp.float32)
    part = KEY_BLOCK // RUNS
    kv = kv.reshape(RUNS, token_rows // part, part, 2 * split).transpose(1, 0, 2, 3).reshape(RUNS * token_rows, 2 * split)
    out = attention(
        query,
        kv,
        runs,
        mine.astype(jnp.float32)[None, :],
        pos.astype(jnp.float32)[:, None],
        segment_ids.reshape(-1, 128),
    )
    return out[None]


def solution(mesh):
    placed = (P("dp", "ctx", None), P("dp", "ctx"), P("dp", None), P("dp", None), P("dp", None), P("dp", None))
    return jax.shard_map(
        shards, mesh=mesh, in_specs=placed, out_specs=P("dp", "ctx", None), check_vma=False
    )
```

time: 437 us -> 335 us (0.77)
  local copies, waits for them, and re-layouts: 81.5 us -> 19 us
  Pallas kernels: 0 us -> 51.2 us
  matrix products: 61.6 us -> 21.3 us
  blocking collectives: 50.4 us -> 26.1 us
  other arithmetic: 27.4 us -> 9.26 us
  waiting for transfers between devices: 200 us -> 195 us
    all_gather x4 -> x2, waiting for transfers between devices: 170 us -> 109 us  [the longest x1 58.4 us: shards(): kv = lax.all_gather(kv.reshape(token_rows, 2 * split), 'ctx', axis=0)]
    all_gather x1, waiting for transfers between devices: 28.4 us -> 85.1 us  [shards(): lax.all_gather(w_query, 'dp', axis=0, tiled=True)]
    pallas_call x0 -> x1, Pallas kernels: none -> 51.2 us  [attention(): pl.pallas_call(attention_kernel, out_shape=jax.ShapeDtypeStruct((TOKENS,...]
    dot_general x27 -> x3, matrix products: 61.6 us -> 21.3 us  [the longest x1 11.1 us: shards(): jnp.dot(flat, lax.all_gather(w_query, 'dp', axis=0, tiled=True), preferre...]
    dot_general x2 -> x0, local copies, waits for them, and re-layouts: 27.3 us -> none  [the longest x1 20.8 us: shards(): jnp.dot(part, lax.all_gather(w_query, 'dp', axis=0, tiled=True), preferre...]
    dynamic_slice x48 -> x0, local copies, waits for them, and re-layouts: 25 us -> none  [the longest x24 13.3 us: one_block(): lax.dynamic_slice_in_dim(values, index * attention_block, attention_block...]
    all_gather x2 -> x1, blocking collectives: 50.4 us -> 26.1 us  [shards(): runs = lax.all_gather(mine, 'ctx', axis=0).astype(jnp.float32)]
    while x60 -> x0, local copies, waits for them, and re-layouts: 23.1 us -> none
  transfers between devices with their start and end apart: 5 -> 3, of which waited for: 5 -> 3; matrix products, arithmetic and copies ran while one was open for 12% -> 5% of each run, Pallas kernels for 0% -> 0%
where the time goes in v1:
time: 335 us
  waiting for transfers between devices  195 us (58%)
  Pallas kernels  51.2 us (15%)
  blocking collectives  26.1 us (8%)
  matrix products  21.3 us (6%)
  local copies, waits for them, and re-layouts  19 us (6%)
  between operations  13.2 us (4%)
  other arithmetic  9.26 us (3%)
    all_gather x1, waiting for transfers between devices, shards(): lax.all_gather(w_query, 'dp', axis=0, tiled=True)  85.1 us
    all_gather x1, waiting for transfers between devices, shards(): kv = lax.all_gather(kv.reshape(token_rows, 2 * split), 'ctx', axis=0)  58.4 us
    pallas_call x1, Pallas kernels, attention(): pl.pallas_call(attention_kernel, out_shape=jax.ShapeDtypeStruct((TOKENS,...  51.2 us
    all_gather x1, waiting for transfers between devices, shards(): lax.all_gather(both, 'dp', axis=0, tiled=True)  50.4 us
    all_gather x1, blocking collectives, shards(): runs = lax.all_gather(mine, 'ctx', axis=0).astype(jnp.float32)  26.1 us
    dot_general x1, matrix products, shards(): jnp.dot(flat, lax.all_gather(w_query, 'dp', axis=0, tiled=True), preferre...  11.1 us
    dot_general x1, matrix products, shards(): jnp.dot(flat, lax.all_gather(both, 'dp', axis=0, tiled=True), preferred_e...  6.76 us
    transpose x1, local copies, waits for them, and re-layouts, shards(): kv.reshape(RUNS, token_rows // part, part, 2 * split).transpose(1, 0, 2, 3)  6.75 us
  transfers between devices with their start and end apart: 3, of which 3 were waited for; matrix products, arithmetic and copies ran while one was open for 5% of the time, Pallas kernels for 0%

profile of v1, /device:TPU:1, one launch (start us, length us, event | category | flops | bytes accessed | tf_op | source)
XLA Modules:
  0.0 334.9 jit_solution(16512934449552657877)
XLA Ops:
  6.5 2.0 pad_maximum_fusion.2
  8.6 0.8 convert_bitcast_fusion
  9.4 0.2 convert_reduce_fusion
  9.6 0.2 select_reduce_fusion
  9.8 1.1 multiply_cosine_fusion
  10.9 3.4 %convolution_convert_fusion = bf16[384,4096]{1,0:T(8,128)(2,1)} fusion(bf16[1,384,4096]{2,1,0:T(8,128)(2,1)S(1)} %copy-done, s32[384]{0:T(512)S(1)} %convert_reduce_fusion), kind=kOutput, calls=%fused_computation | convolution fusion | flops 1209679872 | bytes 6292992 | tf_op jit(solution)/shard_map/dot_general | solution.py:148
  14.4 50.4 %all-gather.8.cloned.1.call-done = bf16[4096,1024]{1,0:T(8,128)(2,1)} async-done(((bf16[256,1024]{1,0:T(8,128)(2,1)}), bf16[4096,1024]{1,0:T(8,128)(2,1)}) %all-gather.8.cloned.1.call-update) | async-done | bytes 8388624 | tf_op jit(solution)/shard_map/all_gather | solution.py:151
  64.8 6.8 %fusion.5 = f32[384,1024]{1,0:T(8,128)S(1)} fusion(bf16[384,4096]{1,0:T(8,128)(2,1)} %convolution_convert_fusion, bf16[4096,1024]{1,0:T(8,128)(2,1)} %all-gather.8.cloned.1.call-done), kind=kOutput, calls=%fused_computation.24 | convolution fusion | flops 3221225472 | bytes 13107200 | tf_op jit(solution)/shard_map/dot_general | solution.py:151
  71.6 0.1 slice.48
  71.6 1.0 slice.27
  72.6 0.9 copy.36
  73.5 2.3 copy.37
  75.9 1.3 fusion.2
  77.2 1.0 pad_maximum_fusion.1
  78.1 2.3 copy.32
  80.5 0.0 all-gather.6.cloned.1.call-start
  80.5 0.7 all-gather.6.cloned.1.call-update
  81.2 1.0 copy.27
  82.2 1.0 copy.26
  83.2 0.6 reshape.130.mine_ref
  83.8 0.8 copy.35.stored_ref
  84.7 26.1 %all-gather.1 = s32[8,1,384]{2,1,0:T(1,128)S(1)} all-gather(s32[1,1,384]{2,1,0:T(1,128)S(1)} %reshape.131), channel_id=2, replica_groups=mesh['dp'=16,'ctx'=8] {'ctx'}, dimensions={0}, use_global_device_ids=true | all-gather | bytes 13824 | tf_op jit(solution)/shard_map/all_gather | solution.py:158
  110.8 0.6 fusion.4.runs_ref
  111.4 58.4 %all-gather.10.cloned.1.call-done = bf16[8,384,1024]{2,1,0:T(8,128)(2,1)} async-done(((bf16[1,384,1024]{2,1,0:T(8,128)(2,1)}), bf16[8,384,1024]{2,1,0:T(8,128)(2,1)}) %all-gather.10.cloned.1.call-update) | async-done | bytes 6291472 | tf_op jit(solution)/shard_map/all_gather | solution.py:157
  169.8 6.8 %copy.33 = bf16[12,8,32,1024]{3,2,1,0:T(8,128)(2,1)} copy(bf16[12,8,32,1024]{3,2,0,1:T(8,128)(2,1)} %bitcast.34) | data formatting | bytes 12582912 | tf_op jit(solution)/shard_map/transpose | solution.py:160
  176.6 85.1 %all-gather.6.cloned.1.call-done = bf16[4096,2048]{1,0:T(8,128)(2,1)} async-done(((bf16[256,2048]{1,0:T(8,128)(2,1)}), bf16[4096,2048]{1,0:T(8,128)(2,1)}) %all-gather.6.cloned.1.call-update) | async-done | bytes 16777232 | tf_op jit(solution)/shard_map/all_gather | solution.py:149
  261.7 11.1 %convolution_bitcast_fusion = f32[48,8,16,128]{3,1,2,0:T(8,128)S(1)} fusion(bf16[384,4096]{1,0:T(8,128)(2,1)} %convolution_convert_fusion, bf16[4096,2048]{1,0:T(8,128)(2,1)} %all-gather.6.cloned.1.call-done), kind=kOutput, calls=%fused_computation.4 | convolution fusion | flops 6442450944 | bytes 23068672 | tf_op jit(solution)/shard_map/dot_general | solution.py:149
  272.9 0.7 copy.38
  273.5 1.3 subtract_convert_fusion
  274.8 0.9 pad_maximum_fusion
  275.7 1.6 copy.44
  277.2 51.2 %attention.1 = bf16[384,2048]{1,0:T(8,128)(2,1)} custom-call(bf16[384,2048]{1,0:T(8,128)(2,1)} %bitcast.39, bf16[3072,1024]{1,0:T(8,128)(2,1)} %bitcast.35, f32[8,384]{1,0:T(8,128)} %fusion.4.runs_ref, f32[1,384]{1,0:T(1,128)} %reshape.130.mine_ref, f32[384,1]{1,0:T(8,128)} %copy.35.stored_ref, s32[24,128]{1,0:T(8,128)} %bitcast.41), custom_call_target="tpu_custom_call" | custom-call | flops 5000000000 | bytes 11000000 | tf_op jit(solution)/shard_map/attention/pallas_call | solution.py:123
  (11 shorter events, 0.1 us)
Async XLA Ops:
  6.5 4.4 %copy-start = (bf16[1,384,4096]{2,1,0:T(8,128)(2,1)S(1)}, bf16[1,384,4096]{2,1,0:T(8,128)(2,1)}, u32[]{:S(2)}) copy-start(bf16[1,384,4096]{2,1,0:T(8,128)(2,1)} %param.6) | copy-start | bytes 9437188
  6.5 58.3 %all-gather.8.cloned.1.call-start = ((), (), s32[]{:S(2)}) async-start(), calls=%async_computation.1 | async-start | bytes 8912896 | tf_op jit(solution)/shard_map/all_gather | solution.py:151
  8.6 161.3 %all-gather.10.cloned.1.call-start = ((), (), s32[]{:S(2)}) async-start(), calls=%async_computation.2 | async-start | bytes 7077888 | tf_op jit(solution)/shard_map/all_gather | solution.py:157
  73.5 3.6 %copy-start.1 = (bf16[384,512]{0,1:T(8,128)(2,1)S(1)}, bf16[384,512]{0,1:T(8,128)(2,1)}, u32[]{:S(2)}) copy-start(bf16[384,512]{0,1:T(8,128)(2,1)} %copy.36) | copy-start | bytes 1179652
  80.5 181.3 %all-gather.6.cloned.1.call-start = ((), (), s32[]{:S(2)}) async-start(), calls=%async_computation | async-start | bytes 17825792 | tf_op jit(solution)/shard_map/all_gather | solution.py:149
Sparse Core Ops, SparseCore 0:
  9.1 55.7 all-gather.7
  80.6 89.2 all-gather.9
  171.6 90.1 all-gather.5

commit v2 on v1

v2 whole, which is shorter than its diff:
```python
import math

import jax
import jax.numpy as jnp
from jax import lax
from jax.experimental import pallas as pl
from jax.experimental.pallas import tpu as pltpu
from jax.sharding import PartitionSpec as P

QUERY_HEADS = 16
KEY_VALUE_HEADS = 4
HEAD_SIZE = 128
DOCS = 8


RUNS = 8
TOKENS = 384
KEY_BLOCK = 256
QUERY_TILE = 64
GROUP = 4
NEVER = -1e30


def attention_kernel(q_ref, kv_ref, runs_ref, stored_ref, seg_ref, out_ref, key_pos, top, total, summed, rows_done):
    part = KEY_BLOCK // RUNS
    blocks = TOKENS // part
    tiles = TOKENS // QUERY_TILE
    width = GROUP * QUERY_TILE
    factor = HEAD_SIZE ** -0.5 * math.log2(math.e)

    query_pos = runs_ref[lax.axis_index("ctx")][:1]
    seg = seg_ref[...]
    start = jnp.zeros_like(query_pos)
    for doc in range(1, DOCS):
        before = jnp.sum((seg < doc).astype(jnp.float32), axis=1, keepdims=True)
        start = jnp.where(before <= query_pos, jnp.maximum(start, before), start)

    runs = runs_ref[:, 0]
    columns = runs.T
    for run in range(RUNS):
        wide = jnp.broadcast_to(columns[:, run : run + 1], (TOKENS, 128))
        key_pos[:, run] = wide.reshape(blocks, part, 128)

    lane = lax.broadcasted_iota(jnp.int32, (1, TOKENS), 1) % part
    lowest = jnp.where(lane == 0, jnp.min(runs, axis=0, keepdims=True), 1e9)
    highest = jnp.where(lane == part - 1, jnp.max(runs, axis=0, keepdims=True), 1e9)

    for tile in range(tiles):
        at = slice(tile * QUERY_TILE, (tile + 1) * QUERY_TILE)
        pos_row = jnp.concatenate([query_pos[:, at]] * GROUP, axis=1)
        start_row = jnp.concatenate([start[:, at]] * GROUP, axis=1)
        last = jnp.max(query_pos[:, at], axis=1, keepdims=True)
        first = jnp.min(start[:, at], axis=1, keepdims=True)
        begin = jnp.sum((highest < first).astype(jnp.int32))
        end = jnp.sum((lowest <= last).astype(jnp.int32))
        top[...] = jnp.full_like(top, NEVER)
        total[...] = jnp.zeros_like(total)
        summed[...] = jnp.zeros_like(summed)
        queries = [
            jnp.concatenate(
                [q_ref[head * GROUP + g, at] for g in range(GROUP)],
                axis=0,
            )
            for head in range(KEY_VALUE_HEADS)
        ]

        def one_block(block, carry):
            rows = pl.ds(pl.multiple_of(block * KEY_BLOCK, KEY_BLOCK), KEY_BLOCK)
            pos = key_pos[block].reshape(KEY_BLOCK, 128)
            pos = jnp.concatenate([pos] * (width // 128), axis=1)
            visible = (pos <= pos_row) & (pos >= start_row)
            for head in range(KEY_VALUE_HEADS):
                keys = kv_ref[head, rows, :HEAD_SIZE]
                values = kv_ref[head, rows, HEAD_SIZE:]
                score = lax.dot_general(
                    keys, queries[head], (((1,), (1,)), ((), ())), preferred_element_type=jnp.float32
                )
                score = jnp.where(visible, score, -jnp.inf)
                old = top[head]
                new = jnp.maximum(old, jnp.max(score, axis=0, keepdims=True))
                weight = jnp.exp2((score - new) * factor)
                fade = jnp.exp2((old - new) * factor)
                top[head] = new
                total[head] = total[head] * fade + jnp.sum(weight, axis=0, keepdims=True)
                added = lax.dot_general(
                    values, weight.astype(jnp.bfloat16), (((0,), (0,)), ((), ())), preferred_element_type=jnp.float32
                )
                summed[head] = summed[head] * fade + added
            return carry

        lax.fori_loop(begin, end, one_block, 0)
        for head in range(KEY_VALUE_HEADS):
            result = (summed[head] / total[head]).astype(jnp.bfloat16)
            for g in range(GROUP):
                rows_done[head * GROUP + g, :, at] = result[:, g * QUERY_TILE : (g + 1) * QUERY_TILE]

    stored = jnp.broadcast_to(stored_ref[...].astype(jnp.float32), (8, TOKENS)).T[:, :1]
    turn = (stored == query_pos).astype(jnp.bfloat16)
    for head in range(QUERY_HEADS):
        out_ref[:, head * HEAD_SIZE : (head + 1) * HEAD_SIZE] = lax.dot_general(
            turn, rows_done[head], (((1,), (1,)), ((), ())), preferred_element_type=jnp.float32
        ).astype(jnp.bfloat16)


def attention(query, kv, runs, stored, seg):
    part = KEY_BLOCK // RUNS
    width = GROUP * QUERY_TILE
    return pl.pallas_call(
        attention_kernel,
        out_shape=jax.ShapeDtypeStruct((TOKENS, QUERY_HEADS * HEAD_SIZE), jnp.bfloat16),
        in_specs=[pl.BlockSpec(memory_space=pltpu.VMEM)] * 5,
        out_specs=pl.BlockSpec(memory_space=pltpu.VMEM),
        scratch_shapes=[
            pltpu.VMEM((TOKENS // part, RUNS, part, 128), jnp.float32),
            pltpu.VMEM((KEY_VALUE_HEADS, 1, width), jnp.float32),
            pltpu.VMEM((KEY_VALUE_HEADS, 1, width), jnp.float32),
            pltpu.VMEM((KEY_VALUE_HEADS, HEAD_SIZE, width), jnp.float32),
            pltpu.VMEM((QUERY_HEADS, HEAD_SIZE, TOKENS), jnp.bfloat16),
        ],
        compiler_params=pltpu.CompilerParams(vmem_limit_bytes=56 << 20),
        cost_estimate=pl.CostEstimate(flops=5 * 10**9, bytes_accessed=11 * 10**6, transcendentals=10**7),
        name="attention",
    )(query, kv, runs, stored, seg)


ROWS = 256
CHIPS = 8
CHUNK = 2 * ROWS
COPIES = 128
PART = KEY_BLOCK // RUNS
BLOCKS = TOKENS // PART


def projection_kernel(
    tokens, positions, freq, w_query, w_key, w_value,
    q_out, kv_out, pos_out,
    stored, tok, weights_a, weights_b, weights_c, weights_d,
    acc_a, acc_b, acc_c, acc_d, tables, kv_stage, q_stage, pos_stage,
    local_sem, send_sem, recv_sem,
):
    dp, ctx = lax.axis_index("dp"), lax.axis_index("ctx")
    core, x, y_lo = dp % 2, (dp // 2) % 4, dp // 8
    y_hi, z = ctx // 4, ctx % 4
    other = 1 - core

    def device(core=core, x=x, y_lo=y_lo, y_hi=y_hi, z=z):
        return ((y_lo * 4 + x) * 2 + core, y_hi * 4 + z)

    right, left, across = (x + 1) % 4, (x + 3) % 4, (x + 2) % 4
    z_right, z_left = (z + 1) % 4, (z + 3) % 4
    far = 1 - y_lo
    y_up = device(y_lo=far, y_hi=(y_hi + y_lo) % 2)
    y_down = device(y_lo=far, y_hi=(y_hi + far) % 2)
    x_up, x_down = device(x=right), device(x=left)
    z_up, z_down = device(z=z_right), device(z=z_left)
    sibling = device(core=other)
    opposite = device(y_hi=1 - y_hi)

    locals_, copies = [], []

    def local(src, dst):
        copy = pltpu.make_async_copy(src, dst, local_sem.at[len(locals_)])
        locals_.append(copy)
        copy.start()
        return copy

    def remote(src, dst, to):
        at = len(copies)
        copy = pltpu.make_async_remote_copy(
            src_ref=src, dst_ref=dst, send_sem=send_sem.at[at], recv_sem=recv_sem.at[at],
            device_id=to, device_id_type=pl.DeviceIdType.MESH,
        )
        copies.append(copy)
        copy.start()
        return copy

    def chip(x, row=y_lo):
        return row * 4 + x

    def columns(ref, start, size):
        return ref.at[:, pl.ds(pl.multiple_of(start, size), size)]

    me = chip(x)
    half = HEAD_SIZE
    buffers = (weights_a, weights_b, weights_c, weights_d)
    totals = (acc_a, acc_b, acc_c, acc_d)

    def sources(piece, of_core):
        if piece < 2:
            start = (of_core * 2 + piece) * half
            return [(columns(w_key, start, half), slice(0, half)), (columns(w_value, start, half), slice(half, 2 * half))]
        start = (of_core * 2 + piece - 2) * 4 * half
        return [(columns(w_query, start, 4 * half), slice(0, 4 * half))]

    own = [[local(src, buffers[p].at[me, core, :, to]) for src, to in sources(p, core)] for p in (0, 1)]
    read = local(tokens, stored)
    own += [[local(src, buffers[p].at[me, core, :, to]) for src, to in sources(p, core)] for p in (2, 3)]

    barrier = pltpu.get_barrier_semaphore()
    partners = (sibling, x_up, x_down, y_up, y_down, z_up, z_down, opposite)
    for partner in partners:
        pl.semaphore_signal(barrier, inc=1, device_id=partner, device_id_type=pl.DeviceIdType.MESH)
    pl.semaphore_wait(barrier, len(partners))

    def to_sibling(piece):
        return [remote(src, buffers[piece].at[me, core, :, to], sibling) for src, to in sources(piece, other)]

    def unit(piece, at, row, to):
        ref = buffers[piece].at[at, row]
        return remote(ref, ref, to)

    def send_x(piece, at, row):
        return unit(piece, at, row, x_up), unit(piece, at, row, x_down)

    def send_y(piece, at):
        return unit(piece, at, core, y_up), unit(piece, at, other, y_down)

    def arrive(*some):
        for copy in some:
            copy.wait_recv()

    def add(piece, at, first=False):
        weights = buffers[piece][at]
        product = jnp.dot(
            tok[at], weights.reshape(CHUNK, weights.shape[-1]), preferred_element_type=jnp.float32
        )
        if first:
            totals[piece][...] = product
        else:
            totals[piece][...] += product

    sib = [to_sibling(0), to_sibling(1)]
    x1, y1 = {}, {}

    def start_x(piece, row):
        for copy in own[piece]:
            copy.wait()
        x1[piece] = [send_x(piece, row, core)]

    def finish_x(piece, row):
        arrive(*sib[piece])
        x1[piece].append(send_x(piece, row, other))

    for piece in (0, 1):
        start_x(piece, me)
    for piece in (0, 1):
        finish_x(piece, me)
        y1[piece] = {0: send_y(piece, me)}
    sib += [to_sibling(2), to_sibling(3)]

    pos_row = positions[...].astype(jnp.float32)
    pos_col = jnp.broadcast_to(pos_row, (8, TOKENS)).T[:, :1]
    rank_row = jnp.sum((pos_col < pos_row).astype(jnp.float32), axis=0, keepdims=True)
    rank_col = jnp.sum((pos_row < pos_col).astype(jnp.float32), axis=1, keepdims=True)
    count_row = lax.broadcasted_iota(jnp.int32, (TOKENS, TOKENS), 1).astype(jnp.float32)
    count_col = lax.broadcasted_iota(jnp.int32, (TOKENS, TOKENS), 0).astype(jnp.float32)
    turn = count_col == rank_row
    sorted_col = jnp.sum(jnp.where(turn, pos_row, 0.0), axis=1, keepdims=True)
    sorted_row = jnp.sum(jnp.where(count_row == rank_col, pos_col, 0.0), axis=0, keepdims=True)
    pos_stage[...] = jnp.broadcast_to(sorted_row, (8, TOKENS))
    run = ctx
    local(pos_stage, pos_out.at[run])
    pos_z = [remote(pos_stage, pos_out.at[run], z_up), remote(pos_stage, pos_out.at[run], z_down)]
    pos_y = remote(pos_stage, pos_out.at[run], opposite)
    turn = turn.astype(jnp.bfloat16)
    read.wait()
    sent_tokens = []
    for at in range(CHIPS):
        tok[at, :TOKENS] = jnp.dot(
            turn, stored[:, at * CHUNK : (at + 1) * CHUNK], preferred_element_type=jnp.float32
        ).astype(jnp.bfloat16)
        if at % 4 == 3:
            some = pl.ds(at - 3, 4)
            sent_tokens.append(remote(tok.at[some, pl.ds(0, TOKENS)], tok.at[some, pl.ds(TOKENS, TOKENS)], sibling))
    angle = sorted_col * freq[...]
    sign = jnp.where(lax.broadcasted_iota(jnp.int32, (1, HEAD_SIZE), 1) < HEAD_SIZE // 2, -1.0, 1.0)
    tables[0, 0] = jnp.cos(angle)
    tables[0, 1] = jnp.sin(angle) * sign
    sent_tables = remote(tables.at[0], tables.at[1], sibling)

    def neighbours_x(piece, row, with_y):
        (up, down), (up2, down2) = x1[piece]
        arrive(up, up2)
        second = [unit(piece, chip(left, row), core, x_up)]
        if with_y:
            y1[piece][3] = send_y(piece, chip(left, row))
        arrive(down, down2)
        second.append(unit(piece, chip(right, row), other, x_down))
        if with_y:
            y1[piece][1] = send_y(piece, chip(right, row))
        return second

    def across_x(piece, second):
        arrive(*second)
        y1[piece][2] = send_y(piece, chip(across))

    def rotate(value, which):
        return value * tables[which, 0] + pltpu.roll(value, HEAD_SIZE // 2, 1) * tables[which, 1]

    z1, y2, kv_sib, z2 = {}, {}, {}, {}

    def kv_block(head, of_run, part=slice(None)):
        return kv_out.at[head, part, of_run]

    def head_of(piece, whose):
        return (core if whose == 0 else other) * 2 + piece

    def send_kv(piece, whose):
        head = head_of(piece, whose)
        dst = kv_block(head, run)
        src = kv_stage.at[piece, 0] if whose == 0 else dst
        z1[piece, whose] = remote(src, dst, z_up), remote(src, dst, z_down)
        y2[piece, whose] = remote(src, dst, opposite)

    def pass_z(piece, whose, of_y, from_z1):
        head = head_of(piece, whose)
        arrive(*from_z1)
        low, high = pl.ds(0, BLOCKS // 2), pl.ds(BLOCKS // 2, BLOCKS // 2)
        a = kv_block(head, of_y * 4 + z_left, low)
        b = kv_block(head, of_y * 4 + z_right, high)
        return remote(a, a, z_up), remote(b, b, z_down)

    def pass_y(piece, whose):
        arrive(y2[piece, whose])
        ref = kv_block(head_of(piece, whose), (1 - y_hi) * 4 + z)
        return remote(ref, ref, z_up), remote(ref, ref, z_down)

    def finish_kv(piece):
        for s in range(2):
            rows = slice(s * TOKENS, (s + 1) * TOKENS)
            key = rotate(totals[piece][rows, :HEAD_SIZE], s).astype(jnp.bfloat16)
            value = totals[piece][rows, HEAD_SIZE:].astype(jnp.bfloat16)
            kv_stage[piece, s] = jnp.concatenate([key, value], axis=1).reshape(BLOCKS, PART, 2 * HEAD_SIZE)
        dst = kv_block(head_of(piece, 0), run)
        kv_sib[piece] = remote(kv_stage.at[piece, 1], dst, sibling)
        local(kv_stage.at[piece, 0], dst)
        send_kv(piece, 0)

    def second_kv(piece):
        arrive(kv_sib[piece])
        send_kv(piece, 1)

    def finish_q(piece):
        j = piece - 2
        for s in range(2):
            for g in range(4):
                rows = slice(s * TOKENS, (s + 1) * TOKENS)
                cols = slice(g * HEAD_SIZE, (g + 1) * HEAD_SIZE)
                q_stage[j, s, g] = rotate(totals[piece][rows, cols], s).astype(jnp.bfloat16)
        dst = q_out.at[pl.ds((core * 2 + j) * 4, 4)]
        local(q_stage.at[j, 0], dst)
        return remote(q_stage.at[j, 1], dst, sibling)

    second = neighbours_x(0, y_lo, True)
    arrive(*sent_tokens)
    add(0, me, True)
    add(0, chip(left))
    add(0, chip(right))
    across_x(0, second)
    second = neighbours_x(1, y_lo, True)
    start_x(2, me)
    finish_x(2, me)
    arrive(*sib[3])
    for copy in own[3]:
        copy.wait()
    q1_y = send_y(3, me)
    y1[2] = {0: send_y(2, me)}
    add(0, chip(across))
    arrive(*y1[0][0], *y1[0][1], *y1[0][3])
    add(0, chip(x, far))
    add(0, chip(left, far))
    add(0, chip(right, far))
    arrive(*y1[0][2])
    add(0, chip(across, far))
    arrive(sent_tables)
    finish_kv(0)
    pos_z2 = []
    arrive(*pos_z)
    ref = pos_out.at[y_hi * 4 + z_left]
    pos_z2.append(remote(ref, ref, z_up))
    arrive(pos_y)
    ref = pos_out.at[(1 - y_hi) * 4 + z]
    pos_far = [remote(ref, ref, z_up), remote(ref, ref, z_down)]

    across_x(1, second)
    add(1, me, True)
    add(1, chip(left))
    add(1, chip(right))
    add(1, chip(across))
    second_kv(0)
    arrive(*y1[1][0], *y1[1][1], *y1[1][3])
    add(1, chip(x, far))
    add(1, chip(left, far))
    add(1, chip(right, far))
    second = neighbours_x(2, y_lo, True)
    x1[3] = [send_x(3, me, core), send_x(3, me, other)]
    arrive(*y1[1][2])
    add(1, chip(across, far))
    finish_kv(1)
    z2[0, 0] = pass_z(0, 0, y_hi, z1[0, 0])
    z2[0, 1] = pass_z(0, 1, y_hi, z1[0, 1])
    second_kv(1)
    f1, f2 = {}, {}
    for whose in (0, 1):
        f1[0, whose] = pass_y(0, whose)

    across_x(2, second)
    add(2, me, True)
    add(2, chip(left))
    add(2, chip(right))
    add(2, chip(across))
    arrive(*pos_far)
    ref = pos_out.at[(1 - y_hi) * 4 + z_left]
    pos_far2 = remote(ref, ref, z_up)
    arrive(*q1_y)
    there = chip(x, far)
    second = neighbours_x(3, y_lo, False)
    x1[4] = [send_x(3, there, core), send_x(3, there, other)]
    for whose in (0, 1):
        f2[0, whose] = pass_z(0, whose, 1 - y_hi, f1[0, whose])
    for whose in (0, 1):
        z2[1, whose] = pass_z(1, whose, y_hi, z1[1, whose])
        f1[1, whose] = pass_y(1, whose)
    arrive(*y1[2][0], *y1[2][1], *y1[2][3])
    add(2, chip(x, far))
    add(2, chip(left, far))
    add(2, chip(right, far))
    arrive(*y1[2][2])
    add(2, chip(across, far))
    q_copies = [finish_q(2)]

    add(3, me, True)
    add(3, there)
    add(3, chip(left))
    add(3, chip(right))
    arrive(*second)
    add(3, chip(across))
    for whose in (0, 1):
        f2[1, whose] = pass_z(1, whose, 1 - y_hi, f1[1, whose])
    (up, down), (up2, down2) = x1[4]
    arrive(up, up2)
    second = [unit(3, chip(left, far), core, x_up)]
    arrive(down, down2)
    second.append(unit(3, chip(right, far), other, x_down))
    add(3, chip(left, far))
    add(3, chip(right, far))
    arrive(*second)
    add(3, chip(across, far))
    q_copies.append(finish_q(3))

    arrive(*pos_z2, pos_far2)
    for key in z2:
        arrive(*z2[key], *f2[key])
    arrive(*q_copies)
    for copy in copies:
        copy.wait_send()
    for copy in locals_[len(locals_) - 5 :]:
        copy.wait()


def projections(tokens, positions, freq, w_query, w_key, w_value):
    anywhere = pl.BlockSpec(memory_space=pl.ANY)
    vmem = pl.BlockSpec(memory_space=pltpu.VMEM)
    wide = 4 * HEAD_SIZE
    return pl.pallas_call(
        projection_kernel,
        out_shape=[
            jax.ShapeDtypeStruct((QUERY_HEADS, TOKENS, HEAD_SIZE), jnp.bfloat16),
            jax.ShapeDtypeStruct((KEY_VALUE_HEADS, BLOCKS, RUNS, PART, 2 * HEAD_SIZE), jnp.bfloat16),
            jax.ShapeDtypeStruct((RUNS, 8, TOKENS), jnp.float32),
        ],
        in_specs=[anywhere, vmem, vmem, anywhere, anywhere, anywhere],
        out_specs=[anywhere] * 3,
        scratch_shapes=[
            pltpu.VMEM((TOKENS, CHIPS * CHUNK), jnp.bfloat16),
            pltpu.VMEM((CHIPS, 2 * TOKENS, CHUNK), jnp.bfloat16),
            pltpu.VMEM((CHIPS, 2, ROWS, 2 * HEAD_SIZE), jnp.bfloat16),
            pltpu.VMEM((CHIPS, 2, ROWS, 2 * HEAD_SIZE), jnp.bfloat16),
            pltpu.VMEM((CHIPS, 2, ROWS, wide), jnp.bfloat16),
            pltpu.VMEM((CHIPS, 2, ROWS, wide), jnp.bfloat16),
            pltpu.VMEM((2 * TOKENS, 2 * HEAD_SIZE), jnp.float32),
            pltpu.VMEM((2 * TOKENS, 2 * HEAD_SIZE), jnp.float32),
            pltpu.VMEM((2 * TOKENS, wide), jnp.float32),
            pltpu.VMEM((2 * TOKENS, wide), jnp.float32),
            pltpu.VMEM((2, 2, TOKENS, HEAD_SIZE), jnp.float32),
            pltpu.VMEM((2, 2, BLOCKS, PART, 2 * HEAD_SIZE), jnp.bfloat16),
            pltpu.VMEM((2, 2, 4, TOKENS, HEAD_SIZE), jnp.bfloat16),
            pltpu.VMEM((8, TOKENS), jnp.float32),
            pltpu.SemaphoreType.DMA((16,)),
            pltpu.SemaphoreType.DMA((COPIES,)),
            pltpu.SemaphoreType.DMA((COPIES,)),
        ],
        compiler_params=pltpu.CompilerParams(
            collective_id=0, has_side_effects=True, vmem_limit_bytes=56 << 20
        ),
        cost_estimate=pl.CostEstimate(flops=10**10, bytes_accessed=2 * 10**7, transcendentals=10**5),
        name="projections",
    )(tokens, positions, freq, w_query, w_key, w_value)


def shards(tokens, positions, segment_ids, w_query, key_weight, value_weight):
    half = HEAD_SIZE // 2
    freq = 500000.0 ** (-jnp.arange(half, dtype=jnp.float32) / half)
    freq = jnp.concatenate([freq, freq])[None, :]
    query, kv, runs = projections(tokens[0], positions, freq, w_query, key_weight, value_weight)
    kv = kv.reshape(KEY_VALUE_HEADS, RUNS * TOKENS, 2 * HEAD_SIZE)
    return attention(query, kv, runs, positions, segment_ids)[None]


def solution(mesh):
    placed = (P("dp", "ctx", None), P("dp", "ctx"), P("dp", None), P("dp", None), P("dp", None), P("dp", None))
    return jax.shard_map(
        shards, mesh=mesh, in_specs=placed, out_specs=P("dp", "ctx", None), check_vma=False
    )
```

time: 335 us -> 160 us (0.48)
  waiting for transfers between devices: 195 us -> 0 us
  Pallas kernels: 51.2 us -> 159 us
  blocking collectives: 26.1 us -> 0 us
  matrix products: 21.3 us -> 0 us
  local copies, waits for them, and re-layouts: 19 us -> 0 us
  between operations: 13.2 us -> 0.01 us
  other arithmetic: 9.26 us -> 0.6 us
    all_gather x3 -> x0, waiting for transfers between devices: 194 us -> none  [the longest x1 85.1 us: shards(): lax.all_gather(w_query, 'dp', axis=0, tiled=True)]
    pallas_call x0 -> x1, Pallas kernels: none -> 110 us  [projections(): pl.pallas_call(projection_kernel, out_shape=[jax.ShapeDtypeStruct((QUERY_...]
    all_gather x1 -> x0, blocking collectives: 26.1 us -> none  [shards(): runs = lax.all_gather(mine, 'ctx', axis=0).astype(jnp.float32)]
    dot_general x3 -> x0, matrix products: 21.3 us -> none  [the longest x1 11.1 us: shards(): jnp.dot(flat, lax.all_gather(w_query, 'dp', axis=0, tiled=True), preferre...]
    transpose x1 -> x0, local copies, waits for them, and re-layouts: 6.75 us -> none  [shards(): kv.reshape(RUNS, token_rows // part, part, 2 * split).transpose(1, 0, 2, 3)]
    concatenate x3 -> x0, other arithmetic: 4.15 us -> none  [the longest x2 2.13 us: apply_rotary(): jnp.concatenate([first * cosine - second * sine, second * cosine + first...]
  transfers between devices with their start and end apart: 3 -> 0, of which waited for: 3 -> 0; matrix products, arithmetic and copies ran while one was open for 5% -> 0% of each run, Pallas kernels for 0% -> 0%
where the time goes in v2:
time: 160 us
  Pallas kernels  159 us (99%)
    pallas_call x1, Pallas kernels, projections(): pl.pallas_call(projection_kernel, out_shape=[jax.ShapeDtypeStruct((QUERY_...  110 us
    pallas_call x1, Pallas kernels, attention(): pl.pallas_call(attention_kernel, out_shape=jax.ShapeDtypeStruct((TOKENS,...  49.7 us

profile of v2, /device:TPU:1, one launch (start us, length us, event | category | flops | bytes accessed | tf_op | source)
XLA Modules:
  0.0 159.8 jit_solution(16501878004734506560)
XLA Ops:
  0.0 0.6 maximum_bitcast_fusion.freq
  0.6 109.5 %projections.1 = (bf16[16,384,128]{2,1,0:T(8,128)(2,1)}, bf16[4,12,8,32,256]{4,3,2,1,0:T(8,128)(2,1)}, f32[8,8,384]{2,1,0:T(8,128)}) custom-call(bf16[384,4096]{1,0:T(8,128)(2,1)} %bitcast.5, s32[1,384]{1,0:T(1,128)} %stored_ref.1, f32[1,128]{1,0:T(1,128)} %maximum_bitcast_fusion.freq, bf16[256,2048]{1,0:T(8,128)(2,1)} %w_query.1, bf16[256,512]{1,0:T(8,128)(2,1)} %w_key.1, ...), custom_call_target="tpu_custom_call" | custom-call | flops 10000000000 | bytes 20000000 | tf_op jit(solution)/shard_map/projections/pallas_call | solution.py:465
  110.1 49.7 %attention.1 = bf16[384,2048]{1,0:T(8,128)(2,1)} custom-call(bf16[16,384,128]{2,1,0:T(8,128)(2,1)} %get-tuple-element.8.q_ref, bf16[4,3072,256]{2,1,0:T(8,128)(2,1)} %bitcast.6, f32[8,8,384]{2,1,0:T(8,128)} %get-tuple-element.10.runs_ref, s32[1,384]{1,0:T(1,128)} %stored_ref.1, s32[1,3072]{1,0:T(1,128)} %seg_ref.1), custom_call_target="tpu_custom_call" | custom-call | flops 5000000000 | bytes 11000000 | tf_op jit(solution)/shard_map/attention/pallas_call | solution.py:108
  (1 shorter events, 0.0 us)

commit v3 on v2

--- a/solution.py
+++ b/solution.py
@@ -16,12 +16,12 @@
 RUNS = 8
 TOKENS = 384
 KEY_BLOCK = 256
-QUERY_TILE = 64
+QUERY_TILE = 96
 GROUP = 4
 NEVER = -1e30
 
 
-def attention_kernel(q_ref, kv_ref, runs_ref, stored_ref, seg_ref, out_ref, key_pos, top, total, summed, rows_done):
+def attention_kernel(q_ref, kv_ref, runs_ref, stored_ref, seg_ref, out_ref, key_pos, top, total, summed, rows_done, qp, qs):
     part = KEY_BLOCK // RUNS
     blocks = TOKENS // part
     tiles = TOKENS // QUERY_TILE
@@ -36,10 +36,10 @@
         start = jnp.where(before <= query_pos, jnp.maximum(start, before), start)
 
     runs = runs_ref[:, 0]
-    columns = runs.T
-    for run in range(RUNS):
-        wide = jnp.broadcast_to(columns[:, run : run + 1], (TOKENS, 128))
-        key_pos[:, run] = wide.reshape(blocks, part, 128)
+    for block in range(blocks):
+        key_pos[block] = jnp.concatenate([runs[run : run + 1, block * part : (block + 1) * part] for run in range(RUNS)], axis=1)
+    qp[...] = jnp.broadcast_to(jnp.broadcast_to(query_pos, (8, TOKENS)).T[:, :1], (TOKENS, 128))
+    qs[...] = jnp.broadcast_to(jnp.broadcast_to(start, (8, TOKENS)).T[:, :1], (TOKENS, 128))
 
     lane = lax.broadcasted_iota(jnp.int32, (1, TOKENS), 1) % part
     lowest = jnp.where(lane == 0, jnp.min(runs, axis=0, keepdims=True), 1e9)
@@ -47,8 +47,6 @@
 
     for tile in range(tiles):
         at = slice(tile * QUERY_TILE, (tile + 1) * QUERY_TILE)
-        pos_row = jnp.concatenate([query_pos[:, at]] * GROUP, axis=1)
-        start_row = jnp.concatenate([start[:, at]] * GROUP, axis=1)
         last = jnp.max(query_pos[:, at], axis=1, keepdims=True)
         first = jnp.min(start[:, at], axis=1, keepdims=True)
         begin = jnp.sum((highest < first).astype(jnp.int32))
@@ -66,39 +64,41 @@
 
         def one_block(block, carry):
             rows = pl.ds(pl.multiple_of(block * KEY_BLOCK, KEY_BLOCK), KEY_BLOCK)
-            pos = key_pos[block].reshape(KEY_BLOCK, 128)
-            pos = jnp.concatenate([pos] * (width // 128), axis=1)
-            visible = (pos <= pos_row) & (pos >= start_row)
+            pos = key_pos[block]
+            q_at = jnp.concatenate([qp[at]] * (KEY_BLOCK // 128), axis=1)
+            s_at = jnp.concatenate([qs[at]] * (KEY_BLOCK // 128), axis=1)
+            visible = (pos <= q_at) & (pos >= s_at)
+            visible = jnp.concatenate([visible] * GROUP, axis=0)
+            scores = [lax.dot_general(queries[head], kv_ref[head, rows, :HEAD_SIZE], (((1,), (1,)), ((), ())), preferred_element_type=jnp.float32) for head in range(KEY_VALUE_HEADS)]
+            weights=[]; fades=[]
             for head in range(KEY_VALUE_HEADS):
-                keys = kv_ref[head, rows, :HEAD_SIZE]
-                values = kv_ref[head, rows, HEAD_SIZE:]
-                score = lax.dot_general(
-                    keys, queries[head], (((1,), (1,)), ((), ())), preferred_element_type=jnp.float32
-                )
-                score = jnp.where(visible, score, -jnp.inf)
+                SC = scores[head]
+                score = jnp.where(visible, SC, -jnp.inf)
                 old = top[head]
-                new = jnp.maximum(old, jnp.max(score, axis=0, keepdims=True))
-                weight = jnp.exp2((score - new) * factor)
+                new = jnp.maximum(old, jnp.max(score, axis=1, keepdims=True))
+                wide = jnp.concatenate([new] * (KEY_BLOCK // 128), axis=1)
+                weight = jnp.exp2((score - wide) * factor)
                 fade = jnp.exp2((old - new) * factor)
                 top[head] = new
-                total[head] = total[head] * fade + jnp.sum(weight, axis=0, keepdims=True)
-                added = lax.dot_general(
-                    values, weight.astype(jnp.bfloat16), (((0,), (0,)), ((), ())), preferred_element_type=jnp.float32
-                )
-                summed[head] = summed[head] * fade + added
+                total[head] = total[head] * fade + weight[:, :128] + weight[:, 128:]
+                weight = weight.astype(jnp.bfloat16)
+                weights.append(weight); fades.append(fade)
+            for head in range(KEY_VALUE_HEADS):
+                added = jnp.dot(weights[head], kv_ref[head, rows, HEAD_SIZE:], preferred_element_type=jnp.float32)
+                summed[head] = summed[head] * fades[head] + added
             return carry
 
         lax.fori_loop(begin, end, one_block, 0)
         for head in range(KEY_VALUE_HEADS):
-            result = (summed[head] / total[head]).astype(jnp.bfloat16)
+            result = (summed[head] / jnp.sum(total[head], axis=1, keepdims=True)).astype(jnp.bfloat16)
             for g in range(GROUP):
-                rows_done[head * GROUP + g, :, at] = result[:, g * QUERY_TILE : (g + 1) * QUERY_TILE]
+                rows_done[head * GROUP + g, at] = result[g * QUERY_TILE : (g + 1) * QUERY_TILE]
 
     stored = jnp.broadcast_to(stored_ref[...].astype(jnp.float32), (8, TOKENS)).T[:, :1]
     turn = (stored == query_pos).astype(jnp.bfloat16)
     for head in range(QUERY_HEADS):
         out_ref[:, head * HEAD_SIZE : (head + 1) * HEAD_SIZE] = lax.dot_general(
-            turn, rows_done[head], (((1,), (1,)), ((), ())), preferred_element_type=jnp.float32
+            turn, rows_done[head], (((1,), (0,)), ((), ())), preferred_element_type=jnp.float32
         ).astype(jnp.bfloat16)
 
 
@@ -111,11 +111,13 @@
         in_specs=[pl.BlockSpec(memory_space=pltpu.VMEM)] * 5,
         out_specs=pl.BlockSpec(memory_space=pltpu.VMEM),
         scratch_shapes=[
-            pltpu.VMEM((TOKENS // part, RUNS, part, 128), jnp.float32),
-            pltpu.VMEM((KEY_VALUE_HEADS, 1, width), jnp.float32),
-            pltpu.VMEM((KEY_VALUE_HEADS, 1, width), jnp.float32),
-            pltpu.VMEM((KEY_VALUE_HEADS, HEAD_SIZE, width), jnp.float32),
-            pltpu.VMEM((QUERY_HEADS, HEAD_SIZE, TOKENS), jnp.bfloat16),
+            pltpu.VMEM((TOKENS // part, 1, KEY_BLOCK), jnp.float32),
+            pltpu.VMEM((KEY_VALUE_HEADS, width, 128), jnp.float32),
+            pltpu.VMEM((KEY_VALUE_HEADS, width, 128), jnp.float32),
+            pltpu.VMEM((KEY_VALUE_HEADS, width, HEAD_SIZE), jnp.float32),
+            pltpu.VMEM((QUERY_HEADS, TOKENS, HEAD_SIZE), jnp.bfloat16),
+            pltpu.VMEM((TOKENS, 128), jnp.float32),
+            pltpu.VMEM((TOKENS, 128), jnp.float32),
         ],
         compiler_params=pltpu.CompilerParams(vmem_limit_bytes=56 << 20),
         cost_estimate=pl.CostEstimate(flops=5 * 10**9, bytes_accessed=11 * 10**6, transcendentals=10**7),
@@ -126,7 +128,7 @@
 ROWS = 256
 CHIPS = 8
 CHUNK = 2 * ROWS
-COPIES = 128
+COPIES = 144
 PART = KEY_BLOCK // RUNS
 BLOCKS = TOKENS // PART
 
@@ -205,9 +207,14 @@
     def to_sibling(piece):
         return [remote(src, buffers[piece].at[me, core, :, to], sibling) for src, to in sources(piece, other)]
 
+    mine = pl.ds(pl.multiple_of((z % 2) * (ROWS // 2), ROWS // 2), ROWS // 2)
+
     def unit(piece, at, row, to):
-        ref = buffers[piece].at[at, row]
+        ref = buffers[piece].at[at, row, mine] if piece == 0 else buffers[piece].at[at, row]
         return remote(ref, ref, to)
+
+    def send_z(at):
+        return unit(0, at, core, z_up), unit(0, at, other, z_down)
 
     def send_x(piece, at, row):
         return unit(piece, at, row, x_up), unit(piece, at, row, x_down)
@@ -229,24 +236,20 @@
         else:
             totals[piece][...] += product
 
-    sib = [to_sibling(0), to_sibling(1)]
-    x1, y1 = {}, {}
-
-    def start_x(piece, row):
+    sib, x1, y1, by_z = {}, {}, {}, []
+
+    def start(piece):
         for copy in own[piece]:
             copy.wait()
-        x1[piece] = [send_x(piece, row, core)]
-
-    def finish_x(piece, row):
+        x1[piece] = [send_x(piece, me, core)]
+        up = unit(piece, me, core, y_up)
         arrive(*sib[piece])
-        x1[piece].append(send_x(piece, row, other))
-
-    for piece in (0, 1):
-        start_x(piece, me)
-    for piece in (0, 1):
-        finish_x(piece, me)
-        y1[piece] = {0: send_y(piece, me)}
-    sib += [to_sibling(2), to_sibling(3)]
+        x1[piece].append(send_x(piece, me, other))
+        y1[piece] = {0: (up, unit(piece, me, other, y_down))}
+
+    sib[0] = to_sibling(0)
+    start(0)
+    sib[1] = to_sibling(1)
 
     pos_row = positions[...].astype(jnp.float32)
     pos_col = jnp.broadcast_to(pos_row, (8, TOKENS)).T[:, :1]
@@ -284,15 +287,21 @@
         second = [unit(piece, chip(left, row), core, x_up)]
         if with_y:
             y1[piece][3] = send_y(piece, chip(left, row))
+        if piece == 0:
+            by_z.append(send_z(chip(left)))
         arrive(down, down2)
         second.append(unit(piece, chip(right, row), other, x_down))
         if with_y:
             y1[piece][1] = send_y(piece, chip(right, row))
+        if piece == 0:
+            by_z.append(send_z(chip(right)))
         return second
 
     def across_x(piece, second):
         arrive(*second)
         y1[piece][2] = send_y(piece, chip(across))
+        if piece == 0:
+            by_z.append(send_z(chip(across)))
 
     def rotate(value, which):
         return value * tables[which, 0] + pltpu.roll(value, HEAD_SIZE // 2, 1) * tables[which, 1]
@@ -352,28 +361,39 @@
         return remote(q_stage.at[j, 1], dst, sibling)
 
     second = neighbours_x(0, y_lo, True)
+    start(1)
+    sib[2], sib[3] = to_sibling(2), to_sibling(3)
+    across_x(0, second)
+    for which, there in ((0, x), (3, left), (1, right)):
+        arrive(*y1[0][which])
+        by_z.append(send_z(chip(there, far)))
     arrive(*sent_tokens)
     add(0, me, True)
-    add(0, chip(left))
-    add(0, chip(right))
-    across_x(0, second)
+    for at, there in enumerate((left, right, across)):
+        arrive(*by_z[at])
+        add(0, chip(there))
+    arrive(*y1[0][2])
+    by_z.append(send_z(chip(across, far)))
     second = neighbours_x(1, y_lo, True)
-    start_x(2, me)
-    finish_x(2, me)
-    arrive(*sib[3])
+    start(2)
+    for at, there in enumerate((x, left, right, across)):
+        arrive(*by_z[at + 3])
+        add(0, chip(there, far))
+    arrive(sent_tables)
+    finish_kv(0)
+    across_x(1, second)
+    second_kv(0)
+
     for copy in own[3]:
         copy.wait()
+    arrive(*sib[3])
     q1_y = send_y(3, me)
-    y1[2] = {0: send_y(2, me)}
-    add(0, chip(across))
-    arrive(*y1[0][0], *y1[0][1], *y1[0][3])
-    add(0, chip(x, far))
-    add(0, chip(left, far))
-    add(0, chip(right, far))
-    arrive(*y1[0][2])
-    add(0, chip(across, far))
-    arrive(sent_tables)
-    finish_kv(0)
+    add(1, me, True)
+    add(1, chip(left))
+    add(1, chip(right))
+    add(1, chip(across))
+    second = neighbours_x(2, y_lo, True)
+    x1[3] = [send_x(3, me, core), send_x(3, me, other)]
     pos_z2 = []
     arrive(*pos_z)
     ref = pos_out.at[y_hi * 4 + z_left]
@@ -381,28 +401,19 @@
     arrive(pos_y)
     ref = pos_out.at[(1 - y_hi) * 4 + z]
     pos_far = [remote(ref, ref, z_up), remote(ref, ref, z_down)]
-
-    across_x(1, second)
-    add(1, me, True)
-    add(1, chip(left))
-    add(1, chip(right))
-    add(1, chip(across))
-    second_kv(0)
+    z2[0, 0] = pass_z(0, 0, y_hi, z1[0, 0])
+    z2[0, 1] = pass_z(0, 1, y_hi, z1[0, 1])
+    f1, f2 = {}, {}
+    for whose in (0, 1):
+        f1[0, whose] = pass_y(0, whose)
     arrive(*y1[1][0], *y1[1][1], *y1[1][3])
     add(1, chip(x, far))
     add(1, chip(left, far))
     add(1, chip(right, far))
-    second = neighbours_x(2, y_lo, True)
-    x1[3] = [send_x(3, me, core), send_x(3, me, other)]
     arrive(*y1[1][2])
     add(1, chip(across, far))
     finish_kv(1)
-    z2[0, 0] = pass_z(0, 0, y_hi, z1[0, 0])
-    z2[0, 1] = pass_z(0, 1, y_hi, z1[0, 1])
     second_kv(1)
-    f1, f2 = {}, {}
-    for whose in (0, 1):
-        f1[0, whose] = pass_y(0, whose)
 
     across_x(2, second)
     add(2, me, True)

time: 160 us -> 123 us (0.77); the launches traced: 160 us -> 121 us
  Pallas kernels: 159 us -> 120 us
    pallas_call x1, Pallas kernels: 49.7 us -> 27.2 us  [attention(): pl.pallas_call(attention_kernel, out_shape=jax.ShapeDtypeStruct((TOKENS,...]
    pallas_call x1, Pallas kernels: 110 us -> 93.1 us  [projections(): pl.pallas_call(projection_kernel, out_shape=[jax.ShapeDtypeStruct((QUERY_...]
where the time goes in v3:
time: 123 us; the launch traced here: 121 us
  Pallas kernels  120 us (98%)
    pallas_call x1, Pallas kernels, projections(): pl.pallas_call(projection_kernel, out_shape=[jax.ShapeDtypeStruct((QUERY_...  93.1 us
    pallas_call x1, Pallas kernels, attention(): pl.pallas_call(attention_kernel, out_shape=jax.ShapeDtypeStruct((TOKENS,...  27.2 us

profile of v3, /device:TPU:1, one launch (start us, length us, event | category | flops | bytes accessed | tf_op | source)
XLA Modules:
  0.0 120.9 jit_solution(10393688904933897843)
XLA Ops:
  0.0 0.6 maximum_bitcast_fusion.freq
  0.6 93.1 %projections.1 = (bf16[16,384,128]{2,1,0:T(8,128)(2,1)}, bf16[4,12,8,32,256]{4,3,2,1,0:T(8,128)(2,1)}, f32[8,8,384]{2,1,0:T(8,128)}) custom-call(bf16[384,4096]{1,0:T(8,128)(2,1)} %bitcast.5, s32[1,384]{1,0:T(1,128)} %stored_ref.1, f32[1,128]{1,0:T(1,128)} %maximum_bitcast_fusion.freq, bf16[256,2048]{1,0:T(8,128)(2,1)} %w_query.1, bf16[256,512]{1,0:T(8,128)(2,1)} %w_key.1, ...), custom_call_target="tpu_custom_call" | custom-call | flops 10000000000 | bytes 20000000 | tf_op jit(solution)/shard_map/projections/pallas_call | solution.py:476
  93.7 27.2 %attention.1 = bf16[384,2048]{1,0:T(8,128)(2,1)} custom-call(bf16[16,384,128]{2,1,0:T(8,128)(2,1)} %get-tuple-element.8.q_ref, bf16[4,3072,256]{2,1,0:T(8,128)(2,1)} %bitcast.6, f32[8,8,384]{2,1,0:T(8,128)} %get-tuple-element.10.runs_ref, s32[1,384]{1,0:T(1,128)} %stored_ref.1, s32[1,3072]{1,0:T(1,128)} %seg_ref.1), custom_call_target="tpu_custom_call" | custom-call | flops 5000000000 | bytes 11000000 | tf_op jit(solution)/shard_map/attention/pallas_call | solution.py:108
  (1 shorter events, 0.0 us)

commit v4 on v3

v4 whole, which is shorter than its diff:
```python
import math

import jax
import jax.numpy as jnp
from jax import lax
from jax.experimental import pallas as pl
from jax.experimental.pallas import tpu as pltpu
from jax.sharding import PartitionSpec as P

QUERY_HEADS = 16
KEY_VALUE_HEADS = 4
HEAD_SIZE = 128
DOCS = 8


RUNS = 8
TOKENS = 384
KEY_BLOCK = 256
QUERY_TILE = 96
GROUP = 4
NEVER = -1e30


def attention_kernel(
    q_hbm, kv_hbm, runs_ref, stored_ref, seg_ref, out_ref,
    q_ref, kv_ref, key_pos, query_at, start_at, top, total, summed, rows_done, sem,
):
    part = KEY_BLOCK // RUNS
    blocks = TOKENS // part
    tiles = TOKENS // QUERY_TILE
    factor = HEAD_SIZE ** -0.5 * math.log2(math.e)
    loads = [pltpu.make_async_copy(q_hbm, q_ref, sem.at[0]), pltpu.make_async_copy(kv_hbm, kv_ref, sem.at[1])]
    for load in loads:
        load.start()

    query_pos = runs_ref[lax.axis_index("ctx")][:1]
    seg = seg_ref[...]
    start = jnp.zeros_like(query_pos)
    for doc in range(1, DOCS):
        before = jnp.sum((seg < doc).astype(jnp.float32), axis=1, keepdims=True)
        start = jnp.where(before <= query_pos, jnp.maximum(start, before), start)

    runs = runs_ref[:, 0]
    for block in range(blocks):
        at = slice(block * part, (block + 1) * part)
        key_pos[block] = jnp.concatenate([runs[run : run + 1, at] for run in range(RUNS)], axis=1)
    query_at[...] = jnp.broadcast_to(jnp.broadcast_to(query_pos, (8, TOKENS)).T[:, :1], (TOKENS, 128))
    start_at[...] = jnp.broadcast_to(jnp.broadcast_to(start, (8, TOKENS)).T[:, :1], (TOKENS, 128))

    lane = lax.broadcasted_iota(jnp.int32, (1, TOKENS), 1) % part
    lowest = jnp.where(lane == 0, jnp.min(runs, axis=0, keepdims=True), 1e9)
    highest = jnp.where(lane == part - 1, jnp.max(runs, axis=0, keepdims=True), 1e9)
    ranges = []
    for tile in range(tiles):
        at = slice(tile * QUERY_TILE, (tile + 1) * QUERY_TILE)
        last = jnp.max(query_pos[:, at], axis=1, keepdims=True)
        first = jnp.min(start[:, at], axis=1, keepdims=True)
        ranges.append((jnp.sum((highest < first).astype(jnp.int32)), jnp.sum((lowest <= last).astype(jnp.int32))))
    for load in loads:
        load.wait()

    for tile in range(tiles):
        at = slice(tile * QUERY_TILE, (tile + 1) * QUERY_TILE)
        begin, end = ranges[tile]
        top[...] = jnp.full_like(top, NEVER)
        total[...] = jnp.zeros_like(total)
        summed[...] = jnp.zeros_like(summed)
        queries = [
            jnp.concatenate([q_ref[head * GROUP + g, at] for g in range(GROUP)], axis=0)
            for head in range(KEY_VALUE_HEADS)
        ]

        def step(block, count):
            rows = pl.ds(pl.multiple_of(block * KEY_BLOCK, KEY_BLOCK), count * KEY_BLOCK)
            pos = jnp.concatenate([key_pos[block + i] for i in range(count)], axis=1)
            lanes = count * KEY_BLOCK // 128
            visible = (pos <= jnp.concatenate([query_at[at]] * lanes, axis=1)) & (
                pos >= jnp.concatenate([start_at[at]] * lanes, axis=1)
            )
            visible = jnp.concatenate([visible] * GROUP, axis=0)
            scores = [
                lax.dot_general(
                    queries[head], kv_ref[head, rows, :HEAD_SIZE], (((1,), (1,)), ((), ())),
                    preferred_element_type=jnp.float32,
                )
                for head in range(KEY_VALUE_HEADS)
            ]
            weights, fades = [], []
            for head in range(KEY_VALUE_HEADS):
                score = jnp.where(visible, scores[head], -jnp.inf)
                old = top[head]
                new = jnp.maximum(old, jnp.max(score, axis=1, keepdims=True))
                weight = jnp.exp2((score - jnp.concatenate([new] * lanes, axis=1)) * factor)
                fade = jnp.exp2((old - new) * factor)
                top[head] = new
                total[head] = total[head] * fade + sum(weight[:, i * 128 : (i + 1) * 128] for i in range(lanes))
                weights.append(weight.astype(jnp.bfloat16))
                fades.append(fade)
            for head in range(KEY_VALUE_HEADS):
                added = jnp.dot(weights[head], kv_ref[head, rows, HEAD_SIZE:], preferred_element_type=jnp.float32)
                summed[head] = summed[head] * fades[head] + added

        pairs = (end - begin) // 2

        @pl.loop(0, pairs)
        def _(pair):
            step(begin + 2 * pair, 2)

        @pl.loop(begin + 2 * pairs, end)
        def _(block):
            step(block, 1)

        for head in range(KEY_VALUE_HEADS):
            result = (summed[head] / jnp.sum(total[head], axis=1, keepdims=True)).astype(jnp.bfloat16)
            for g in range(GROUP):
                cols = slice((head * GROUP + g) * HEAD_SIZE, (head * GROUP + g + 1) * HEAD_SIZE)
                rows_done[at, cols] = result[g * QUERY_TILE : (g + 1) * QUERY_TILE]

    stored = jnp.broadcast_to(stored_ref[...].astype(jnp.float32), (8, TOKENS)).T[:, :1]
    turn = (stored == query_pos).astype(jnp.bfloat16)
    wide = 4 * HEAD_SIZE
    for at in range(0, QUERY_HEADS * HEAD_SIZE, wide):
        out_ref[:, at : at + wide] = jnp.dot(
            turn, rows_done[:, at : at + wide], preferred_element_type=jnp.float32
        ).astype(jnp.bfloat16)


def attention(query, kv, runs, stored, seg):
    part = KEY_BLOCK // RUNS
    width = GROUP * QUERY_TILE
    vmem = pl.BlockSpec(memory_space=pltpu.VMEM)
    anywhere = pl.BlockSpec(memory_space=pl.ANY)
    return pl.pallas_call(
        attention_kernel,
        out_shape=jax.ShapeDtypeStruct((TOKENS, QUERY_HEADS * HEAD_SIZE), jnp.bfloat16),
        in_specs=[anywhere, anywhere, vmem, vmem, vmem],
        out_specs=vmem,
        scratch_shapes=[
            pltpu.VMEM((QUERY_HEADS, TOKENS, HEAD_SIZE), jnp.bfloat16),
            pltpu.VMEM((KEY_VALUE_HEADS, RUNS * TOKENS, 2 * HEAD_SIZE), jnp.bfloat16),
            pltpu.VMEM((TOKENS // part, 1, KEY_BLOCK), jnp.float32),
            pltpu.VMEM((TOKENS, 128), jnp.float32),
            pltpu.VMEM((TOKENS, 128), jnp.float32),
            pltpu.VMEM((KEY_VALUE_HEADS, width, 128), jnp.float32),
            pltpu.VMEM((KEY_VALUE_HEADS, width, 128), jnp.float32),
            pltpu.VMEM((KEY_VALUE_HEADS, width, HEAD_SIZE), jnp.float32),
            pltpu.VMEM((TOKENS, QUERY_HEADS * HEAD_SIZE), jnp.bfloat16),
            pltpu.SemaphoreType.DMA((2,)),
        ],
        compiler_params=pltpu.CompilerParams(vmem_limit_bytes=56 << 20),
        cost_estimate=pl.CostEstimate(flops=5 * 10**9, bytes_accessed=11 * 10**6, transcendentals=10**7),
        name="attention",
    )(query, kv, runs, stored, seg)


ROWS = 256
CHIPS = 8
CHUNK = 2 * ROWS
COPIES = 144
PART = KEY_BLOCK // RUNS
BLOCKS = TOKENS // PART


def projection_kernel(
    tokens, positions, freq, w_query, w_key, w_value,
    q_out, kv_out, pos_out,
    stored, tok, weights_a, weights_b, weights_c, weights_d,
    acc_a, acc_b, acc_c, acc_d, tables, kv_stage, q_stage, pos_stage,
    local_sem, send_sem, recv_sem,
):
    dp, ctx = lax.axis_index("dp"), lax.axis_index("ctx")
    core, x, y_lo = dp % 2, (dp // 2) % 4, dp // 8
    y_hi, z = ctx // 4, ctx % 4
    other = 1 - core

    def device(core=core, x=x, y_lo=y_lo, y_hi=y_hi, z=z):
        return ((y_lo * 4 + x) * 2 + core, y_hi * 4 + z)

    right, left, across = (x + 1) % 4, (x + 3) % 4, (x + 2) % 4
    z_right, z_left = (z + 1) % 4, (z + 3) % 4
    far = 1 - y_lo
    y_up = device(y_lo=far, y_hi=(y_hi + y_lo) % 2)
    y_down = device(y_lo=far, y_hi=(y_hi + far) % 2)
    x_up, x_down = device(x=right), device(x=left)
    z_up, z_down = device(z=z_right), device(z=z_left)
    sibling = device(core=other)
    opposite = device(y_hi=1 - y_hi)

    locals_, copies = [], []

    def local(src, dst):
        copy = pltpu.make_async_copy(src, dst, local_sem.at[len(locals_)])
        locals_.append(copy)
        copy.start()
        return copy

    def remote(src, dst, to):
        at = len(copies)
        copy = pltpu.make_async_remote_copy(
            src_ref=src, dst_ref=dst, send_sem=send_sem.at[at], recv_sem=recv_sem.at[at],
            device_id=to, device_id_type=pl.DeviceIdType.MESH,
        )
        copies.append(copy)
        copy.start()
        return copy

    def chip(x, row=y_lo):
        return row * 4 + x

    def columns(ref, start, size):
        return ref.at[:, pl.ds(pl.multiple_of(start, size), size)]

    me = chip(x)
    half = HEAD_SIZE
    buffers = (weights_a, weights_b, weights_c, weights_d)
    totals = (acc_a, acc_b, acc_c, acc_d)

    def sources(piece, of_core):
        if piece < 2:
            start = (of_core * 2 + piece) * half
            return [(columns(w_key, start, half), slice(0, half)), (columns(w_value, start, half), slice(half, 2 * half))]
        start = (of_core * 2 + piece - 2) * 4 * half
        return [(columns(w_query, start, 4 * half), slice(0, 4 * half))]

    own = [[local(src, buffers[p].at[me, core, :, to]) for src, to in sources(p, core)] for p in (0, 1)]
    read = local(tokens, stored)
    own += [[local(src, buffers[p].at[me, core, :, to]) for src, to in sources(p, core)] for p in (2, 3)]

    barrier = pltpu.get_barrier_semaphore()
    partners = (sibling, x_up, x_down, y_up, y_down, z_up, z_down, opposite)
    for partner in partners:
        pl.semaphore_signal(barrier, inc=1, device_id=partner, device_id_type=pl.DeviceIdType.MESH)

    pos_row = positions[...].astype(jnp.float32)
    pos_col = jnp.broadcast_to(pos_row, (8, TOKENS)).T[:, :1]
    rank_row = jnp.sum((pos_col < pos_row).astype(jnp.float32), axis=0, keepdims=True)
    rank_col = jnp.sum((pos_row < pos_col).astype(jnp.float32), axis=1, keepdims=True)
    count_row = lax.broadcasted_iota(jnp.int32, (TOKENS, TOKENS), 1).astype(jnp.float32)
    count_col = lax.broadcasted_iota(jnp.int32, (TOKENS, TOKENS), 0).astype(jnp.float32)
    turn = count_col == rank_row
    sorted_col = jnp.sum(jnp.where(turn, pos_row, 0.0), axis=1, keepdims=True)
    sorted_row = jnp.sum(jnp.where(count_row == rank_col, pos_col, 0.0), axis=0, keepdims=True)
    pos_stage[...] = jnp.broadcast_to(sorted_row, (8, TOKENS))
    turn = turn.astype(jnp.bfloat16)
    run = ctx

    pl.semaphore_wait(barrier, len(partners))

    def to_sibling(piece):
        return [remote(src, buffers[piece].at[me, core, :, to], sibling) for src, to in sources(piece, other)]

    mine = pl.ds(pl.multiple_of((z % 2) * (ROWS // 2), ROWS // 2), ROWS // 2)

    def unit(piece, at, row, to):
        ref = buffers[piece].at[at, row, mine] if piece == 0 else buffers[piece].at[at, row]
        return remote(ref, ref, to)

    def send_z(at):
        return unit(0, at, core, z_up), unit(0, at, other, z_down)

    def send_x(piece, at, row):
        return unit(piece, at, row, x_up), unit(piece, at, row, x_down)

    def send_y(piece, at):
        return unit(piece, at, core, y_up), unit(piece, at, other, y_down)

    def arrive(*some):
        for copy in some:
            copy.wait_recv()

    def add(piece, at, first=False):
        weights = buffers[piece][at]
        product = jnp.dot(
            tok[at], weights.reshape(CHUNK, weights.shape[-1]), preferred_element_type=jnp.float32
        )
        if first:
            totals[piece][...] = product
        else:
            totals[piece][...] += product


    def sort_tokens(first):
        for at in range(first, first + 4):
            tok[at, :TOKENS] = jnp.dot(
                turn, stored[:, at * CHUNK : (at + 1) * CHUNK], preferred_element_type=jnp.float32
            ).astype(jnp.bfloat16)
        some = pl.ds(first, 4)
        return remote(tok.at[some, pl.ds(0, TOKENS)], tok.at[some, pl.ds(TOKENS, TOKENS)], sibling)

    x1, x2, y1, by_z, sent_tables, q_copies = {}, {}, {}, {}, [], []
    xs, rows_y = (x, right, across, left), (y_lo, far)

    def forward(piece, k):
        y1[piece, k] = send_y(piece, chip(xs[k]))
        if piece == 0:
            by_z[0, k] = send_z(chip(xs[k]))

    def start_own(piece):
        for copy in own[piece]:
            copy.wait()
        if piece < 3:
            x1[piece, 0] = [send_x(piece, me, core)]
        y1[piece, 0] = [unit(piece, me, core, y_up)]

    def start_other(piece):
        arrive(*sib[piece])
        if piece < 3:
            x1[piece, 0].append(send_x(piece, me, other))
        y1[piece, 0].append(unit(piece, me, other, y_down))

    def start_last():
        x1[3, 0] = [send_x(3, me, core), send_x(3, me, other)]

    def start_far():
        arrive(*y1[3, 0])
        there = chip(x, far)
        x1[3, 1] = [send_x(3, there, core), send_x(3, there, other)]

    def from_left(piece, row):
        arrive(x1[piece, row][0][0], x1[piece, row][1][0])
        x2[piece, row, 0] = unit(piece, chip(left, rows_y[row]), core, x_up)
        if piece < 3:
            forward(piece, 3)

    def from_right(piece, row):
        arrive(x1[piece, row][0][1], x1[piece, row][1][1])
        x2[piece, row, 1] = unit(piece, chip(right, rows_y[row]), other, x_down)
        if piece < 3:
            forward(piece, 1)

    def from_across(piece):
        arrive(x2[piece, 0, 0], x2[piece, 0, 1])
        forward(piece, 2)

    def from_far(k):
        arrive(*y1[0, k])
        by_z[1, k] = send_z(chip(xs[k], far))

    def use(piece, row, k):
        if piece == 0 and (row, k) != (0, 0):
            arrive(*by_z[row, k])
        elif piece in (1, 2) and row == 1:
            arrive(*y1[piece, k])
        elif piece == 3 and k == 2:
            arrive(x2[3, row, 0], x2[3, row, 1])
        if piece == 0 and (row, k) == (0, 0):
            arrive(*sent_tokens)
        add(piece, chip(xs[k], rows_y[row]), (row, k) == (0, 0))

    def make_tables():
        angle = sorted_col * freq[...]
        sign = jnp.where(lax.broadcasted_iota(jnp.int32, (1, HEAD_SIZE), 1) < HEAD_SIZE // 2, -1.0, 1.0)
        tables[0, 0] = jnp.cos(angle)
        tables[0, 1] = jnp.sin(angle) * sign
        sent_tables.append(remote(tables.at[0], tables.at[1], sibling))

    def rotate(value, which):
        return value * tables[which, 0] + pltpu.roll(value, HEAD_SIZE // 2, 1) * tables[which, 1]

    z1, y2, kv_sib, z2, f1, f2 = {}, {}, {}, {}, {}, {}

    def kv_block(head, of_run, part=slice(None)):
        return kv_out.at[head, part, of_run]

    def head_of(piece, whose):
        return (core if whose == 0 else other) * 2 + piece

    def send_kv(piece, whose):
        head = head_of(piece, whose)
        dst = kv_block(head, run)
        src = kv_stage.at[piece, 0] if whose == 0 else dst
        z1[piece, whose] = remote(src, dst, z_up), remote(src, dst, z_down)
        y2[piece, whose] = remote(src, dst, opposite)

    def pass_z(piece, whose, of_y, from_z1):
        head = head_of(piece, whose)
        arrive(*from_z1)
        low, high = pl.ds(0, BLOCKS // 2), pl.ds(BLOCKS // 2, BLOCKS // 2)
        a = kv_block(head, of_y * 4 + z_left, low)
        b = kv_block(head, of_y * 4 + z_right, high)
        return remote(a, a, z_up), remote(b, b, z_down)

    def pass_near(piece, whose):
        z2[piece, whose] = pass_z(piece, whose, y_hi, z1[piece, whose])

    def pass_y(piece, whose):
        arrive(y2[piece, whose])
        ref = kv_block(head_of(piece, whose), (1 - y_hi) * 4 + z)
        f1[piece, whose] = remote(ref, ref, z_up), remote(ref, ref, z_down)

    def pass_far(piece, whose):
        f2[piece, whose] = pass_z(piece, whose, 1 - y_hi, f1[piece, whose])

    pos_z, pos_y, pos_z2 = [], [], []

    def pos_start():
        local(pos_stage, pos_out.at[run])
        pos_z.extend([remote(pos_stage, pos_out.at[run], z_up), remote(pos_stage, pos_out.at[run], z_down)])
        pos_y.append(remote(pos_stage, pos_out.at[run], opposite))

    def pos_near():
        arrive(*pos_z)
        ref = pos_out.at[y_hi * 4 + z_left]
        pos_z2.append(remote(ref, ref, z_up))

    def pos_across():
        arrive(*pos_y)
        ref = pos_out.at[(1 - y_hi) * 4 + z]
        pos_z[:] = [remote(ref, ref, z_up), remote(ref, ref, z_down)]

    def pos_far():
        arrive(*pos_z)
        ref = pos_out.at[(1 - y_hi) * 4 + z_left]
        pos_z2.append(remote(ref, ref, z_up))

    def finish_kv(piece):
        if piece == 0:
            arrive(*sent_tables)
        for s in range(2):
            rows = slice(s * TOKENS, (s + 1) * TOKENS)
            key = rotate(totals[piece][rows, :HEAD_SIZE], s).astype(jnp.bfloat16)
            value = totals[piece][rows, HEAD_SIZE:].astype(jnp.bfloat16)
            kv_stage[piece, s] = jnp.concatenate([key, value], axis=1).reshape(BLOCKS, PART, 2 * HEAD_SIZE)
        dst = kv_block(head_of(piece, 0), run)
        kv_sib[piece] = remote(kv_stage.at[piece, 1], dst, sibling)
        local(kv_stage.at[piece, 0], dst)
        send_kv(piece, 0)

    def second_kv(piece):
        arrive(kv_sib[piece])
        send_kv(piece, 1)

    def finish_q(piece):
        j = piece - 2
        for s in range(2):
            for g in range(4):
                rows = slice(s * TOKENS, (s + 1) * TOKENS)
                cols = slice(g * HEAD_SIZE, (g + 1) * HEAD_SIZE)
                q_stage[j, s, g] = rotate(totals[piece][rows, cols], s).astype(jnp.bfloat16)
        dst = q_out.at[pl.ds((core * 2 + j) * 4, 4)]
        local(q_stage.at[j, 0], dst)
        q_copies.append(remote(q_stage.at[j, 1], dst, sibling))

    sib = [to_sibling(0)]
    start_own(0)
    read.wait()
    sent_tokens = [sort_tokens(0)]
    start_other(0)
    sib.append(to_sibling(1))
    sent_tokens.append(sort_tokens(4))
    sib += [to_sibling(2), to_sibling(3)]

    start_own(3)
    start_own(1)
    from_far(0)
    from_left(0, 0)
    from_right(0, 0)
    pos_start()
    start_other(1)
    make_tables()
    use(0, 0, 0)
    use(1, 0, 0)
    from_across(0)
    start_own(2)
    use(0, 0, 3)
    start_other(3)
    use(0, 1, 0)
    from_left(1, 0)
    pos_near()
    from_far(3)
    from_right(1, 0)
    use(1, 0, 3)
    use(1, 0, 1)
    from_far(1)
    use(3, 0, 0)
    use(1, 1, 0)
    use(0, 0, 2)
    pos_across()
    from_far(2)
    use(0, 1, 3)
    use(0, 0, 1)
    use(0, 1, 1)
    start_last()
    pos_far()
    use(0, 1, 2)
    finish_kv(0)
    from_across(1)
    use(1, 0, 2)
    second_kv(0)
    use(1, 1, 3)
    use(1, 1, 1)
    pass_near(0, 0)
    start_other(2)
    use(2, 0, 0)
    pass_y(0, 0)
    from_left(3, 0)
    from_right(3, 0)
    use(3, 0, 3)
    use(3, 0, 1)
    pass_near(0, 1)
    use(1, 1, 2)
    finish_kv(1)
    second_kv(1)
    from_left(2, 0)
    from_right(2, 0)
    use(2, 0, 1)
    use(2, 0, 3)
    pass_y(0, 1)
    pass_far(0, 0)
    use(2, 1, 0)
    use(3, 0, 2)
    pass_near(1, 0)
    start_far()
    use(3, 1, 0)
    pass_y(1, 0)
    from_across(2)
    use(2, 0, 2)
    pass_near(1, 1)
    pass_y(1, 1)
    pass_far(0, 1)
    use(2, 1, 3)
    from_left(3, 1)
    from_right(3, 1)
    use(3, 1, 3)
    use(3, 1, 1)
    pass_far(1, 0)
    use(2, 1, 1)
    use(2, 1, 2)
    use(3, 1, 2)
    pass_far(1, 1)
    finish_q(3)
    finish_q(2)
    arrive(*pos_z2)
    for key in z2:
        arrive(*z2[key], *f2[key])
    arrive(*q_copies)
    for copy in copies:
        copy.wait_send()
    for copy in locals_[len(locals_) - 5 :]:
        copy.wait()


def projections(tokens, positions, freq, w_query, w_key, w_value):
    anywhere = pl.BlockSpec(memory_space=pl.ANY)
    vmem = pl.BlockSpec(memory_space=pltpu.VMEM)
    wide = 4 * HEAD_SIZE
    return pl.pallas_call(
        projection_kernel,
        out_shape=[
            jax.ShapeDtypeStruct((QUERY_HEADS, TOKENS, HEAD_SIZE), jnp.bfloat16),
            jax.ShapeDtypeStruct((KEY_VALUE_HEADS, BLOCKS, RUNS, PART, 2 * HEAD_SIZE), jnp.bfloat16),
            jax.ShapeDtypeStruct((RUNS, 8, TOKENS), jnp.float32),
        ],
        in_specs=[anywhere, vmem, vmem, anywhere, anywhere, anywhere],
        out_specs=[anywhere] * 3,
        scratch_shapes=[
            pltpu.VMEM((TOKENS, CHIPS * CHUNK), jnp.bfloat16),
            pltpu.VMEM((CHIPS, 2 * TOKENS, CHUNK), jnp.bfloat16),
            pltpu.VMEM((CHIPS, 2, ROWS, 2 * HEAD_SIZE), jnp.bfloat16),
            pltpu.VMEM((CHIPS, 2, ROWS, 2 * HEAD_SIZE), jnp.bfloat16),
            pltpu.VMEM((CHIPS, 2, ROWS, wide), jnp.bfloat16),
            pltpu.VMEM((CHIPS, 2, ROWS, wide), jnp.bfloat16),
            pltpu.VMEM((2 * TOKENS, 2 * HEAD_SIZE), jnp.float32),
            pltpu.VMEM((2 * TOKENS, 2 * HEAD_SIZE), jnp.float32),
            pltpu.VMEM((2 * TOKENS, wide), jnp.float32),
            pltpu.VMEM((2 * TOKENS, wide), jnp.float32),
            pltpu.VMEM((2, 2, TOKENS, HEAD_SIZE), jnp.float32),
            pltpu.VMEM((2, 2, BLOCKS, PART, 2 * HEAD_SIZE), jnp.bfloat16),
            pltpu.VMEM((2, 2, 4, TOKENS, HEAD_SIZE), jnp.bfloat16),
            pltpu.VMEM((8, TOKENS), jnp.float32),
            pltpu.SemaphoreType.DMA((16,)),
            pltpu.SemaphoreType.DMA((COPIES,)),
            pltpu.SemaphoreType.DMA((COPIES,)),
        ],
        compiler_params=pltpu.CompilerParams(
            collective_id=0, has_side_effects=True, vmem_limit_bytes=56 << 20
        ),
        cost_estimate=pl.CostEstimate(flops=10**10, bytes_accessed=2 * 10**7, transcendentals=10**5),
        name="projections",
    )(tokens, positions, freq, w_query, w_key, w_value)


def shards(tokens, positions, segment_ids, w_query, key_weight, value_weight):
    half = HEAD_SIZE // 2
    freq = 500000.0 ** (-jnp.arange(half, dtype=jnp.float32) / half)
    freq = jnp.concatenate([freq, freq])[None, :]
    query, kv, runs = projections(tokens[0], positions, freq, w_query, key_weight, value_weight)
    kv = kv.reshape(KEY_VALUE_HEADS, RUNS * TOKENS, 2 * HEAD_SIZE)
    return attention(query, kv, runs, positions, segment_ids)[None]


def solution(mesh):
    placed = (P("dp", "ctx", None), P("dp", "ctx"), P("dp", None), P("dp", None), P("dp", None), P("dp", None))
    return jax.shard_map(
        shards, mesh=mesh, in_specs=placed, out_specs=P("dp", "ctx", None), check_vma=False
    )
```

time: 123 us -> 112 us (0.911)
  Pallas kernels: 120 us -> 110 us
    pallas_call x1, Pallas kernels: 93.1 us -> 86.9 us  [projections(): pl.pallas_call(projection_kernel, out_shape=[jax.ShapeDtypeStruct((QUERY_...]
    pallas_call x1, Pallas kernels: 27.2 us -> 23.2 us  [attention(): pl.pallas_call(attention_kernel, out_shape=jax.ShapeDtypeStruct((TOKENS,...]
where the time goes in v4:
time: 112 us; the launch traced here: 111 us
  Pallas kernels  110 us (98%)
    pallas_call x1, Pallas kernels, projections(): pl.pallas_call(projection_kernel, out_shape=[jax.ShapeDtypeStruct((QUERY_...  86.9 us
    pallas_call x1, Pallas kernels, attention(): pl.pallas_call(attention_kernel, out_shape=jax.ShapeDtypeStruct((TOKENS,...  23.2 us

profile of v4, /device:TPU:1, one launch (start us, length us, event | category | flops | bytes accessed | tf_op | source)
XLA Modules:
  0.0 110.9 jit_solution(1998268519819350560)
XLA Ops:
  0.0 0.6 maximum_bitcast_fusion.freq
  0.6 86.9 %projections.1 = (bf16[16,384,128]{2,1,0:T(8,128)(2,1)}, bf16[4,12,8,32,256]{4,3,2,1,0:T(8,128)(2,1)}, f32[8,8,384]{2,1,0:T(8,128)}) custom-call(bf16[384,4096]{1,0:T(8,128)(2,1)} %bitcast.5, s32[1,384]{1,0:T(1,128)} %stored_ref.1, f32[1,128]{1,0:T(1,128)} %maximum_bitcast_fusion.freq, bf16[256,2048]{1,0:T(8,128)(2,1)} %w_query.1, bf16[256,512]{1,0:T(8,128)(2,1)} %w_key.1, ...), custom_call_target="tpu_custom_call" | custom-call | flops 10000000000 | bytes 20000000 | tf_op jit(solution)/shard_map/projections/pallas_call | solution.py:547
  87.5 23.2 %attention.1 = bf16[384,2048]{1,0:T(8,128)(2,1)} custom-call(bf16[16,384,128]{2,1,0:T(8,128)(2,1)} %get-tuple-element.8.q_hbm, bf16[4,3072,256]{2,1,0:T(8,128)(2,1)} %bitcast.6, f32[8,8,384]{2,1,0:T(8,128)} %get-tuple-element.10.runs_ref, s32[1,384]{1,0:T(1,128)} %stored_ref.1, s32[1,3072]{1,0:T(1,128)} %seg_ref.1), custom_call_target="tpu_custom_call" | custom-call | flops 5000000000 | bytes 11000000 | tf_op jit(solution)/shard_map/attention/pallas_call | solution.py:133
  (1 shorter events, 0.0 us)

commit v5 on v4

--- a/solution.py
+++ b/solution.py
@@ -2,6 +2,7 @@
 
 import jax
 import jax.numpy as jnp
+import numpy as np
 from jax import lax
 from jax.experimental import pallas as pl
 from jax.experimental.pallas import tpu as pltpu
@@ -100,13 +101,19 @@
                 added = jnp.dot(weights[head], kv_ref[head, rows, HEAD_SIZE:], preferred_element_type=jnp.float32)
                 summed[head] = summed[head] * fades[head] + added
 
-        pairs = (end - begin) // 2
+        fours = (end - begin) // 4
+        rest = begin + 4 * fours
+        pairs = (end - rest) // 2
+
+        @pl.loop(0, fours)
+        def _(four):
+            step(begin + 4 * four, 4)
 
         @pl.loop(0, pairs)
         def _(pair):
-            step(begin + 2 * pair, 2)
-
-        @pl.loop(begin + 2 * pairs, end)
+            step(rest + 2 * pair, 2)
+
+        @pl.loop(rest + 2 * pairs, end)
         def _(block):
             step(block, 1)
 
@@ -414,17 +421,18 @@
         pos_z2.append(remote(ref, ref, z_up))
 
     def finish_kv(piece):
-        if piece == 0:
-            arrive(*sent_tables)
+        dst = kv_block(head_of(piece, 0), run)
         for s in range(2):
+            if s == 1 and piece == 0:
+                arrive(*sent_tables)
             rows = slice(s * TOKENS, (s + 1) * TOKENS)
             key = rotate(totals[piece][rows, :HEAD_SIZE], s).astype(jnp.bfloat16)
             value = totals[piece][rows, HEAD_SIZE:].astype(jnp.bfloat16)
             kv_stage[piece, s] = jnp.concatenate([key, value], axis=1).reshape(BLOCKS, PART, 2 * HEAD_SIZE)
-        dst = kv_block(head_of(piece, 0), run)
+            if s == 0:
+                local(kv_stage.at[piece, 0], dst)
+                send_kv(piece, 0)
         kv_sib[piece] = remote(kv_stage.at[piece, 1], dst, sibling)
-        local(kv_stage.at[piece, 0], dst)
-        send_kv(piece, 0)
 
     def second_kv(piece):
         arrive(kv_sib[piece])
@@ -432,14 +440,15 @@
 
     def finish_q(piece):
         j = piece - 2
-        for s in range(2):
+        dst = q_out.at[pl.ds((core * 2 + j) * 4, 4)]
+        for s in (1, 0):
             for g in range(4):
                 rows = slice(s * TOKENS, (s + 1) * TOKENS)
                 cols = slice(g * HEAD_SIZE, (g + 1) * HEAD_SIZE)
                 q_stage[j, s, g] = rotate(totals[piece][rows, cols], s).astype(jnp.bfloat16)
-        dst = q_out.at[pl.ds((core * 2 + j) * 4, 4)]
+            if s == 1:
+                q_copies.append(remote(q_stage.at[j, 1], dst, sibling))
         local(q_stage.at[j, 0], dst)
-        q_copies.append(remote(q_stage.at[j, 1], dst, sibling))
 
     sib = [to_sibling(0)]
     start_own(0)
@@ -582,8 +591,8 @@
 
 def shards(tokens, positions, segment_ids, w_query, key_weight, value_weight):
     half = HEAD_SIZE // 2
-    freq = 500000.0 ** (-jnp.arange(half, dtype=jnp.float32) / half)
-    freq = jnp.concatenate([freq, freq])[None, :]
+    freq = 500000.0 ** (-(np.arange(HEAD_SIZE) % half) / half)
+    freq = jnp.asarray(freq[None, :], jnp.float32)
     query, kv, runs = projections(tokens[0], positions, freq, w_query, key_weight, value_weight)
     kv = kv.reshape(KEY_VALUE_HEADS, RUNS * TOKENS, 2 * HEAD_SIZE)
     return attention(query, kv, runs, positions, segment_ids)[None]

time: 112 us -> 111 us (level)
  no operation moved by 1% of the time
where the time goes in v5:
time: 111 us; the launch traced here: 109 us
  Pallas kernels  109 us (98%)
    pallas_call x1, Pallas kernels, projections(): pl.pallas_call(projection_kernel, out_shape=[jax.ShapeDtypeStruct((QUERY_...  86.9 us
    pallas_call x1, Pallas kernels, attention(): pl.pallas_call(attention_kernel, out_shape=jax.ShapeDtypeStruct((TOKENS,...  22.4 us

profile of v5, /device:TPU:1, one launch (start us, length us, event | category | flops | bytes accessed | tf_op | source)
XLA Modules:
  0.0 109.5 jit_solution(15081531141358464193)
XLA Ops:
  0.0 86.9 %projections.1 = (bf16[16,384,128]{2,1,0:T(8,128)(2,1)}, bf16[4,12,8,32,256]{4,3,2,1,0:T(8,128)(2,1)}, f32[8,8,384]{2,1,0:T(8,128)}) custom-call(bf16[384,4096]{1,0:T(8,128)(2,1)} %bitcast.3, s32[1,384]{1,0:T(1,128)} %stored_ref.1, f32[1,128]{1,0:T(1,128)} %constant.2.clone.freq, bf16[256,2048]{1,0:T(8,128)(2,1)} %w_query.1, bf16[256,512]{1,0:T(8,128)(2,1)} %w_key.1, ...), custom_call_target="tpu_custom_call" | custom-call | flops 10000000000 | bytes 20000000 | tf_op jit(solution)/shard_map/projections/pallas_call | solution.py:556
  86.9 22.4 %attention.1 = bf16[384,2048]{1,0:T(8,128)(2,1)} custom-call(bf16[16,384,128]{2,1,0:T(8,128)(2,1)} %get-tuple-element.8.q_hbm, bf16[4,3072,256]{2,1,0:T(8,128)(2,1)} %bitcast.4, f32[8,8,384]{2,1,0:T(8,128)} %get-tuple-element.10.runs_ref, s32[1,384]{1,0:T(1,128)} %stored_ref.1, s32[1,3072]{1,0:T(1,128)} %seg_ref.1), custom_call_target="tpu_custom_call" | custom-call | flops 5000000000 | bytes 11000000 | tf_op jit(solution)/shard_map/attention/pallas_call | solution.py:140

commit v6 on v5

--- a/solution.py
+++ b/solution.py
@@ -2,6 +2,7 @@
 
 import jax
 import jax.numpy as jnp
+import ml_dtypes
 import numpy as np
 from jax import lax
 from jax.experimental import pallas as pl
@@ -23,8 +24,8 @@
 
 
 def attention_kernel(
-    q_hbm, kv_hbm, runs_ref, stored_ref, seg_ref, out_ref,
-    q_ref, kv_ref, key_pos, query_at, start_at, top, total, summed, rows_done, sem,
+    q_hbm, kv_hbm, runs_ref, stored_ref, seg_ref, out_hbm,
+    q_ref, kv_ref, key_pos, query_at, start_at, top, total, summed, rows_done, out_ref, sem,
 ):
     part = KEY_BLOCK // RUNS
     blocks = TOKENS // part
@@ -130,6 +131,11 @@
         out_ref[:, at : at + wide] = jnp.dot(
             turn, rows_done[:, at : at + wide], preferred_element_type=jnp.float32
         ).astype(jnp.bfloat16)
+        leave = pltpu.make_async_copy(out_ref.at[:, at : at + wide], out_hbm.at[:, at : at + wide], sem.at[at // wide])
+        leave.start()
+        loads.append(leave)
+    for leave in loads[2:]:
+        leave.wait()
 
 
 def attention(query, kv, runs, stored, seg):
@@ -141,7 +147,7 @@
         attention_kernel,
         out_shape=jax.ShapeDtypeStruct((TOKENS, QUERY_HEADS * HEAD_SIZE), jnp.bfloat16),
         in_specs=[anywhere, anywhere, vmem, vmem, vmem],
-        out_specs=vmem,
+        out_specs=anywhere,
         scratch_shapes=[
             pltpu.VMEM((QUERY_HEADS, TOKENS, HEAD_SIZE), jnp.bfloat16),
             pltpu.VMEM((KEY_VALUE_HEADS, RUNS * TOKENS, 2 * HEAD_SIZE), jnp.bfloat16),
@@ -152,7 +158,8 @@
             pltpu.VMEM((KEY_VALUE_HEADS, width, 128), jnp.float32),
             pltpu.VMEM((KEY_VALUE_HEADS, width, HEAD_SIZE), jnp.float32),
             pltpu.VMEM((TOKENS, QUERY_HEADS * HEAD_SIZE), jnp.bfloat16),
-            pltpu.SemaphoreType.DMA((2,)),
+            pltpu.VMEM((TOKENS, QUERY_HEADS * HEAD_SIZE), jnp.bfloat16),
+            pltpu.SemaphoreType.DMA((4,)),
         ],
         compiler_params=pltpu.CompilerParams(vmem_limit_bytes=56 << 20),
         cost_estimate=pl.CostEstimate(flops=5 * 10**9, bytes_accessed=11 * 10**6, transcendentals=10**7),
@@ -169,7 +176,7 @@
 
 
 def projection_kernel(
-    tokens, positions, freq, w_query, w_key, w_value,
+    tokens, positions, angles, w_query, w_key, w_value,
     q_out, kv_out, pos_out,
     stored, tok, weights_a, weights_b, weights_c, weights_d,
     acc_a, acc_b, acc_c, acc_d, tables, kv_stage, q_stage, pos_stage,
@@ -355,10 +362,16 @@
         add(piece, chip(xs[k], rows_y[row]), (row, k) == (0, 0))
 
     def make_tables():
-        angle = sorted_col * freq[...]
+        high = jnp.floor(sorted_col * (1.0 / 64))
+        lane = lax.broadcasted_iota(jnp.int32, (TOKENS, HEAD_SIZE), 1).astype(jnp.float32)
+        pick = ((lane == high) | (lane == sorted_col - 64 * high + 64)).astype(jnp.bfloat16)
+        terms = jnp.dot(pick, angles[...], preferred_element_type=jnp.float32)
+        size = 4 * HEAD_SIZE
+        both = terms[:, :size] + (terms[:, size : 2 * size] + terms[:, 2 * size :])
+        cos_a, sin_a, cos_b, sin_b = [both[:, k * HEAD_SIZE : (k + 1) * HEAD_SIZE] for k in range(4)]
         sign = jnp.where(lax.broadcasted_iota(jnp.int32, (1, HEAD_SIZE), 1) < HEAD_SIZE // 2, -1.0, 1.0)
-        tables[0, 0] = jnp.cos(angle)
-        tables[0, 1] = jnp.sin(angle) * sign
+        tables[0, 0] = cos_a * cos_b - sin_a * sin_b
+        tables[0, 1] = (sin_a * cos_b + cos_a * sin_b) * sign
         sent_tables.append(remote(tables.at[0], tables.at[1], sibling))
 
     def rotate(value, which):
@@ -549,7 +562,22 @@
         copy.wait()
 
 
-def projections(tokens, positions, freq, w_query, w_key, w_value):
+def angle_terms():
+    half = HEAD_SIZE // 2
+    freq = 500000.0 ** (-(np.arange(HEAD_SIZE) % half) / half)
+    table = np.zeros((128, 4, HEAD_SIZE))
+    coarse = 64 * np.arange(48)[:, None] * freq
+    fine = np.arange(64)[:, None] * freq
+    table[:48, 0], table[:48, 1] = np.cos(coarse), np.sin(coarse)
+    table[64:, 2], table[64:, 3] = np.cos(fine), np.sin(fine)
+    rest, terms = table.reshape(128, 4 * HEAD_SIZE), []
+    for _ in range(3):
+        terms.append(rest.astype(ml_dtypes.bfloat16))
+        rest = rest - terms[-1].astype(np.float64)
+    return jnp.asarray(np.concatenate(terms, axis=1))
+
+
+def projections(tokens, positions, angles, w_query, w_key, w_value):
     anywhere = pl.BlockSpec(memory_space=pl.ANY)
     vmem = pl.BlockSpec(memory_space=pltpu.VMEM)
     wide = 4 * HEAD_SIZE
@@ -586,14 +614,11 @@
         ),
         cost_estimate=pl.CostEstimate(flops=10**10, bytes_accessed=2 * 10**7, transcendentals=10**5),
         name="projections",
-    )(tokens, positions, freq, w_query, w_key, w_value)
+    )(tokens, positions, angles, w_query, w_key, w_value)
 
 
 def shards(tokens, positions, segment_ids, w_query, key_weight, value_weight):
-    half = HEAD_SIZE // 2
-    freq = 500000.0 ** (-(np.arange(HEAD_SIZE) % half) / half)
-    freq = jnp.asarray(freq[None, :], jnp.float32)
-    query, kv, runs = projections(tokens[0], positions, freq, w_query, key_weight, value_weight)
+    query, kv, runs = projections(tokens[0], positions, angle_terms(), w_query, key_weight, value_weight)
     kv = kv.reshape(KEY_VALUE_HEADS, RUNS * TOKENS, 2 * HEAD_SIZE)
     return attention(query, kv, runs, positions, segment_ids)[None]
 

time: 111 us -> 111 us (level)
  no operation moved by 1% of the time
where the time goes in v6:
time: 111 us; the launch traced here: 109 us
  Pallas kernels  109 us (98%)
    pallas_call x1, Pallas kernels, projections(): pl.pallas_call(projection_kernel, out_shape=[jax.ShapeDtypeStruct((QUERY_...  87.3 us
    pallas_call x1, Pallas kernels, attention(): pl.pallas_call(attention_kernel, out_shape=jax.ShapeDtypeStruct((TOKENS,...  21.5 us

profile of v6, /device:TPU:1, one launch (start us, length us, event | category | flops | bytes accessed | tf_op | source)
XLA Modules:
  0.0 109.0 jit_solution(6552591106176065306)
XLA Ops:
  0.0 87.3 %projections.1 = (bf16[16,384,128]{2,1,0:T(8,128)(2,1)}, bf16[4,12,8,32,256]{4,3,2,1,0:T(8,128)(2,1)}, f32[8,8,384]{2,1,0:T(8,128)}) custom-call(bf16[384,4096]{1,0:T(8,128)(2,1)} %bitcast.3, s32[1,384]{1,0:T(1,128)} %stored_ref.1, bf16[128,1536]{1,0:T(8,128)(2,1)} %constant.2.clone.angles, bf16[256,2048]{1,0:T(8,128)(2,1)} %w_query.1, ...), custom_call_target="tpu_custom_call" | custom-call | flops 10000000000 | bytes 20000000 | tf_op jit(solution)/shard_map/projections/pallas_call | solution.py:584
  87.3 21.5 %attention.1 = bf16[384,2048]{1,0:T(8,128)(2,1)} custom-call(bf16[16,384,128]{2,1,0:T(8,128)(2,1)} %get-tuple-element.8.q_hbm, bf16[4,3072,256]{2,1,0:T(8,128)(2,1)} %bitcast.4, f32[8,8,384]{2,1,0:T(8,128)} %get-tuple-element.10.runs_ref, s32[1,384]{1,0:T(1,128)} %stored_ref.1, s32[1,3072]{1,0:T(1,128)} %seg_ref.1), custom_call_target="tpu_custom_call" | custom-call | flops 5000000000 | bytes 11000000 | tf_op jit(solution)/shard_map/attention/pallas_call | solution.py:146
